TPU v7x, 128 devices: a whole 4x4x4 slice. The times are simulated.
128 devices in a mesh: row: 8 (over y, z_lo), col: 16 (over x, z_hi, core).
Axes of the slice: x: 4, y: 4, z: 4 (z_hi: 2, z_lo: 2; z = z_hi * 2 + z_lo), core: 2. Of those that a mesh axis runs over, the one named last changes fastest.
Arguments:
- pair_rep: bfloat16 [512, 512, 128], P('row', 'col'), may hold values from -6 to 6
- side_weight: bfloat16 [2, 2, 2, 128, 128], replicated, may hold values from -0.5 to 0.5
- gate_weight: bfloat16 [2, 128, 128], replicated, may hold values from -0.5 to 0.5
- out_weight: bfloat16 [2, 128, 128], replicated, may hold values from -0.5 to 0.5
- in_gain: float32 [2, 128], replicated, may hold values from 0.1 to 1.9
- out_gain: float32 [2, 128], replicated, may hold values from 0.1 to 1.9
Outputs:
- updated_pair: bfloat16 [512, 512, 128], P('row', 'col')
All inputs are finite; a program needn't handle non-finite values.
Results may differ from a plain program's by a relative error of at most 0.018.
Values may be sent and summed in bfloat16 or wider, within the bound.
No kernel may reach another device: no remote copies, remote signals or barrier semaphores. Data moves between devices by JAX's collectives and lax.ppermute only.
A program may use at most 64 MiB of HBM per device.

v0:
```python
import jax
import jax.numpy as jnp
from jax import lax
from jax.sharding import PartitionSpec as P

epsilon = 1e-05


def layer_norm(values, gain_row, axis_pos):
    average = jnp.mean(values, axis=axis_pos, keepdims=True)
    centred = values - average
    variance = jnp.mean(centred * centred, axis=axis_pos, keepdims=True)
    return centred * lax.rsqrt(variance + epsilon) * gain_row


def to_channels(sides_flat, rows_n, cols_n, tile_rows, tile_cols):
    stack_n, hid_n, flat_n = sides_flat.shape
    moved = lax.all_to_all(sides_flat, ("row", "col"), split_axis=1, concat_axis=2, tiled=True)
    per_dev = moved.shape[1]
    arranged = moved.reshape(stack_n, per_dev, rows_n, cols_n, tile_rows, tile_cols)
    arranged = jnp.transpose(arranged, (0, 1, 2, 4, 3, 5))
    full_sides = arranged.reshape(stack_n, per_dev, rows_n * tile_rows, cols_n * tile_cols)
    return full_sides


def to_tiles(mixed_chan, out_matrix, gain_col, rows_n, cols_n):
    per_dev, full_rows, full_cols = mixed_chan.shape
    tile_rows = full_rows // rows_n
    tile_cols = full_cols // cols_n
    arranged = mixed_chan.reshape(per_dev, rows_n, tile_rows, cols_n, tile_cols)
    arranged = jnp.transpose(arranged, (0, 1, 3, 2, 4)).reshape(
        per_dev, rows_n * cols_n * tile_rows * tile_cols
    )
    returned = lax.all_to_all(arranged, ("row", "col"), split_axis=1, concat_axis=0, tiled=True)
    return (returned, out_matrix, gain_col)


def on_device(pair_rep, side_weight, gate_weight, out_weight, in_gain, out_gain):
    rows_n = lax.axis_size("row")
    cols_n = lax.axis_size("col")
    tile_rows, tile_cols, chan_n = pair_rep.shape
    current = pair_rep.reshape(tile_rows * tile_cols, chan_n)
    for update in range(2):
        normed = layer_norm(current.astype(jnp.float32), in_gain[update], -1).astype(jnp.bfloat16)
        side_list = []
        for side_idx in range(2):
            value_part = jnp.einsum(
                "cd,pc->dp",
                side_weight[update, side_idx, 0],
                normed,
                preferred_element_type=jnp.float32,
            )
            gate_part = jnp.einsum(
                "cd,pc->dp",
                side_weight[update, side_idx, 1],
                normed,
                preferred_element_type=jnp.float32,
            )
            side_list.append((jax.nn.sigmoid(gate_part) * value_part).astype(jnp.bfloat16))
        sides_flat = jnp.stack(side_list, axis=0)
        full_sides = to_channels(sides_flat, rows_n, cols_n, tile_rows, tile_cols)
        if update == 0:
            product_all = jnp.einsum(
                "hik,hjk->hij", full_sides[0], full_sides[1], preferred_element_type=jnp.float32
            )
        else:
            product_all = jnp.einsum(
                "hki,hkj->hij", full_sides[0], full_sides[1], preferred_element_type=jnp.float32
            )
        mixed_chan = product_all.astype(jnp.bfloat16)
        mixed_flat, used_matrix, used_gain = to_tiles(
            mixed_chan, out_weight[update], out_gain[update], rows_n, cols_n
        )
        out_normed = layer_norm(mixed_flat.astype(jnp.float32), used_gain[:, None], 0).astype(
            jnp.bfloat16
        )
        change = jnp.einsum(
            "hp,hd->pd", out_normed, used_matrix, preferred_element_type=jnp.float32
        )
        gate_vals = jax.nn.sigmoid(
            jnp.dot(normed, gate_weight[update], preferred_element_type=jnp.float32)
        )
        current = (current.astype(jnp.float32) + gate_vals * change).astype(jnp.bfloat16)
    return current.reshape(tile_rows, tile_cols, chan_n)


def solution(mesh):
    placed = (P("row", "col", None), P(), P(), P(), P(), P())
    return jax.shard_map(
        on_device, mesh=mesh, in_specs=placed, out_specs=P("row", "col", None), check_vma=False
    )
```

profile of v0, /device:TPU:1, one launch (start us, length us, event | category | flops | bytes accessed | tf_op | source)
XLA Modules:
  0.0 170.6 jit_solution(12226092456684445885)
XLA Ops:
  8.1 30.2 %all_to_all.46 = bf16[2,128,2048]{2,0,1:T(2,128)(2,1)S(1)} all-to-all(bf16[2,128,2048]{2,0,1:T(2,128)(2,1)S(1)} %copy.31), channel_id=1, replica_groups=mesh['row'=8,'col'=16] {'row','col'}, dimensions={1} | all-to-all | bytes 2097152 | tf_op jit(solution)/shard_map/all_to_all | solution.py:18
  38.7 4.5 %reshape.253 = bf16[2,1,8,16,64,32]{5,4,3,2,0,1:T(8,128)(2,1)} reshape(bf16[2,128,2048]{2,1,0:T(8,128)(2,1)S(1)} %copy.32) | data formatting | bytes 2097152 | tf_op jit(solution)/shard_map/reshape | solution.py:20
  43.2 4.9 %fusion.80 = (bf16[1,1,8,64,16,32]{5,3,4,2,0,1:T(8,128)(2,1)S(1)}, bf16[1,1,8,64,16,32]{5,3,4,2,0,1:T(8,128)(2,1)}) fusion(bf16[2,1,8,64,16,32]{5,3,4,2,0,1:T(8,128)(2,1)} %bitcast.136), kind=kLoop, calls=%fused_computation.117 | loop fusion | bytes 2097152 | tf_op jit(solution)/shard_map/slice | solution.py:64
  48.1 2.8 %copy.33 = bf16[1,1,8,64,16,32]{3,2,5,4,1,0:T(8,128)(2,1)} copy(bf16[1,1,8,64,16,32]{5,3,4,2,0,1:T(8,128)(2,1)} %get-tuple-element.8) | data formatting | bytes 1048576 | tf_op jit(solution)/shard_map/slice | solution.py:64
  50.9 1.9 %reshape.254 = bf16[512,512]{0,1:T(8,128)(2,1)S(1)} reshape(bf16[1,1,8,64,16,32]{3,2,5,4,1,0:T(8,128)(2,1)} %copy.33) | data formatting | bytes 1048576 | tf_op jit(solution)/shard_map/reshape.7
  52.8 1.8 %copy.34 = bf16[1,1,8,64,16,32]{3,2,5,4,1,0:T(8,128)(2,1)} copy(bf16[1,1,8,64,16,32]{5,3,4,2,0,1:T(8,128)(2,1)S(1)} %get-tuple-element.7) | data formatting | bytes 1048576 | tf_op jit(solution)/shard_map/slice | solution.py:64
  54.5 1.9 %reshape.255 = bf16[512,512]{0,1:T(8,128)(2,1)S(1)} reshape(bf16[1,1,8,64,16,32]{3,2,5,4,1,0:T(8,128)(2,1)} %copy.34) | data formatting | bytes 1048576 | tf_op jit(solution)/shard_map/reshape.8
  58.6 2.1 %copy.36 = bf16[1,8,16,64,32]{4,3,2,1,0:T(8,128)(2,1)S(1)} copy(bf16[1,8,16,64,32]{3,1,4,2,0:T(8,128)(2,1)} %bitcast.152) | data formatting | bytes 1048576 | tf_op jit(solution)/shard_map/transpose | solution.py:31
  60.7 2.3 %all_to_all.40 = bf16[1,128,2048]{2,0,1:T(2,128)(2,1)} reshape(bf16[1,8,16,64,32]{4,3,2,1,0:T(8,128)(2,1)S(1)} %copy.36) | data formatting | bytes 1048576 | tf_op jit(solution)/shard_map/all_to_all | solution.py:34
  63.6 4.7 %reduce.4 = bf16[128,2048]{1,0:T(8,128)(2,1)S(1)} reduce(bf16[128,1,2048]{2,1,0:T(2,128)(2,1)} %bitcast.150, bf16[]{:T(256)} %broadcast.183), dimensions={1}, to_apply=%bitcast.114.reduce_sub_computation | reduce | bytes 1048578
  69.5 4.6 %all-to-all-start.1 = ((bf16[128,2,1024]{2,1,0:T(2,128)(2,1)}), bf16[128,2,1024]{2,1,0:T(2,128)(2,1)S(1)}, u32[]{:S(2)}, u32[]{:S(2)}) async-start(bf16[128,2,1024]{2,1,0:T(2,128)(2,1)} %reshape.263), calls=%async_computation.1 | async-start | bytes 1048576 | tf_op jit(solution)/shard_map/all_to_all | solution.py:34
  75.5 12.2 %all-to-all-done.1 = bf16[128,2,1024]{2,1,0:T(2,128)(2,1)S(1)} async-done(((bf16[128,2,1024]{2,1,0:T(2,128)(2,1)}), bf16[128,2,1024]{2,1,0:T(2,128)(2,1)S(1)}, u32[]{:S(2)}, u32[]{:S(2)}) %all-to-all-start.1) | async-done | bytes 524320 | tf_op jit(solution)/shard_map/all_to_all | solution.py:34
  93.9 23.0 %all_to_all.47 = bf16[2,128,2048]{2,0,1:T(2,128)(2,1)S(1)} all-to-all(bf16[2,128,2048]{2,0,1:T(2,128)(2,1)S(1)} %copy.39), channel_id=1, replica_groups=mesh['row'=8,'col'=16] {'row','col'}, dimensions={1} | all-to-all | bytes 2097152 | tf_op jit(solution)/shard_map/all_to_all | solution.py:18
  117.3 4.5 %reshape.257 = bf16[2,1,8,16,64,32]{5,4,3,2,0,1:T(8,128)(2,1)} reshape(bf16[2,128,2048]{2,1,0:T(8,128)(2,1)S(1)} %copy.40) | data formatting | bytes 2097152 | tf_op jit(solution)/shard_map/reshape | solution.py:20
  121.7 4.9 %fusion.79 = (bf16[1,1,8,64,16,32]{5,3,4,2,0,1:T(8,128)(2,1)S(1)}, bf16[1,1,8,64,16,32]{5,3,4,2,0,1:T(8,128)(2,1)}) fusion(bf16[2,1,8,64,16,32]{5,3,4,2,0,1:T(8,128)(2,1)} %bitcast.137), kind=kLoop, calls=%fused_computation.116 | loop fusion | bytes 2097152 | tf_op jit(solution)/shard_map/slice | solution.py:68
  126.7 2.8 %copy.41 = bf16[1,1,8,64,16,32]{3,2,5,4,1,0:T(8,128)(2,1)} copy(bf16[1,1,8,64,16,32]{5,3,4,2,0,1:T(8,128)(2,1)} %get-tuple-element.6) | data formatting | bytes 1048576 | tf_op jit(solution)/shard_map/slice | solution.py:68
  129.4 2.6 %reshape.258 = bf16[512,512]{0,1:T(8,128)(2,1)} reshape(bf16[1,1,8,64,16,32]{3,2,5,4,1,0:T(8,128)(2,1)} %copy.41) | data formatting | bytes 1048576 | tf_op jit(solution)/shard_map/reshape.29
  132.0 1.7 %copy.42 = bf16[1,1,8,64,16,32]{3,2,5,4,1,0:T(8,128)(2,1)} copy(bf16[1,1,8,64,16,32]{5,3,4,2,0,1:T(8,128)(2,1)S(1)} %get-tuple-element.5) | data formatting | bytes 1048576 | tf_op jit(solution)/shard_map/slice | solution.py:68
  133.7 1.9 %reshape.259 = bf16[512,512]{0,1:T(8,128)(2,1)S(1)} reshape(bf16[1,1,8,64,16,32]{3,2,5,4,1,0:T(8,128)(2,1)} %copy.42) | data formatting | bytes 1048576 | tf_op jit(solution)/shard_map/reshape.30
  138.9 2.1 %copy.44 = bf16[1,8,16,64,32]{4,3,2,1,0:T(8,128)(2,1)S(1)} copy(bf16[1,8,16,64,32]{3,1,4,2,0:T(8,128)(2,1)} %bitcast.153) | data formatting | bytes 1048576 | tf_op jit(solution)/shard_map/transpose | solution.py:31
  141.0 2.3 %all_to_all.41 = bf16[1,128,2048]{2,0,1:T(2,128)(2,1)} reshape(bf16[1,8,16,64,32]{4,3,2,1,0:T(8,128)(2,1)S(1)} %copy.44) | data formatting | bytes 1048576 | tf_op jit(solution)/shard_map/all_to_all | solution.py:34
  143.3 4.8 %reduce.5 = bf16[128,2048]{1,0:T(8,128)(2,1)S(1)} reduce(bf16[128,1,2048]{2,1,0:T(2,128)(2,1)} %bitcast.151, bf16[]{:T(256)} %broadcast.183), dimensions={1}, to_apply=%bitcast.116.reduce_sub_computation | reduce | bytes 1048578
  149.3 4.6 %all-to-all-start.3 = ((bf16[128,2,1024]{2,1,0:T(2,128)(2,1)}), bf16[128,2,1024]{2,1,0:T(2,128)(2,1)S(1)}, u32[]{:S(2)}, u32[]{:S(2)}) async-start(bf16[128,2,1024]{2,1,0:T(2,128)(2,1)} %reshape.265), calls=%async_computation.3 | async-start | bytes 1048576 | tf_op jit(solution)/shard_map/all_to_all | solution.py:34
  155.3 12.2 %all-to-all-done.3 = bf16[128,2,1024]{2,1,0:T(2,128)(2,1)S(1)} async-done(((bf16[128,2,1024]{2,1,0:T(2,128)(2,1)}), bf16[128,2,1024]{2,1,0:T(2,128)(2,1)S(1)}, u32[]{:S(2)}, u32[]{:S(2)}) %all-to-all-start.3) | async-done | bytes 524320 | tf_op jit(solution)/shard_map/all_to_all | solution.py:34
  (66 shorter events, 28.9 us)
Async XLA Ops:
  0.0 5.6 %copy-start.5 = (bf16[2,2,2,128,128]{4,3,2,1,0:T(8,128)(2,1)S(1)}, bf16[2,2,2,128,128]{4,3,2,1,0:T(8,128)(2,1)}, u32[]{:S(2)}) copy-start(bf16[2,2,2,128,128]{4,3,2,1,0:T(8,128)(2,1)} %param.7) | copy-start | bytes 786436
  63.1 11.0 %copy-start.7 = (f32[2,128]{1,0:T(2,128)S(1)}, f32[2,128]{1,0:T(2,128)}, u32[]{:S(2)}) copy-start(f32[2,128]{1,0:T(2,128)} %param.11) | copy-start | bytes 3076
  63.1 11.0 %copy-start.8 = (bf16[2,128,128]{2,1,0:T(8,128)(2,1)S(1)}, bf16[2,128,128]{2,1,0:T(8,128)(2,1)}, u32[]{:S(2)}) copy-start(bf16[2,128,128]{2,1,0:T(8,128)(2,1)} %param.8) | copy-start | bytes 196612
  69.5 18.3 %all-to-all-start.1 = ((bf16[128,2,1024]{2,1,0:T(2,128)(2,1)}), bf16[128,2,1024]{2,1,0:T(2,128)(2,1)S(1)}, u32[]{:S(2)}, u32[]{:S(2)}) async-start(bf16[128,2,1024]{2,1,0:T(2,128)(2,1)} %reshape.263), calls=%async_computation.1 | async-start | bytes 1048576 | tf_op jit(solution)/shard_map/all_to_all | solution.py:34
  75.5 13.4 %copy-start = (bf16[64,32,128]{2,1,0:T(8,128)(2,1)S(1)}, bf16[64,32,128]{2,1,0:T(8,128)(2,1)}, u32[]{:S(2)}) copy-start(bf16[64,32,128]{2,1,0:T(8,128)(2,1)} %param.6) | copy-start | bytes 1572868
  75.5 13.4 %copy-start.6 = (bf16[2,128,128]{2,1,0:T(8,128)(2,1)S(1)}, bf16[2,128,128]{2,1,0:T(8,128)(2,1)}, u32[]{:S(2)}) copy-start(bf16[2,128,128]{2,1,0:T(8,128)(2,1)} %param.9) | copy-start | bytes 196612
  88.2 1.2 copy-start.3
  91.4 1.2 copy-start.1
  143.3 10.5 %copy-start.2 = (bf16[2048,128]{1,0:T(8,128)(2,1)S(1)}, bf16[2048,128]{1,0:T(8,128)(2,1)}, u32[]{:S(2)}) copy-start(bf16[2048,128]{1,0:T(8,128)(2,1)} %copy-done.1) | copy-start | bytes 1572868
  149.3 18.3 %all-to-all-start.3 = ((bf16[128,2,1024]{2,1,0:T(2,128)(2,1)}), bf16[128,2,1024]{2,1,0:T(2,128)(2,1)S(1)}, u32[]{:S(2)}, u32[]{:S(2)}) async-start(bf16[128,2,1024]{2,1,0:T(2,128)(2,1)} %reshape.265), calls=%async_computation.3 | async-start | bytes 1048576 | tf_op jit(solution)/shard_map/all_to_all | solution.py:34
  168.0 1.2 copy-start.4
where the time goes:
time: 171 us
  local copies, waits for them, and re-layouts  56.6 us (33%)
  blocking collectives  53.2 us (31%)
  waiting for transfers between devices  24.5 us (14%)
  other arithmetic  17.1 us (10%)
  matrix products  9.65 us (6%)
  starting transfers between devices  9.19 us (5%)
    all_to_all x2, blocking collectives, to_channels(): lax.all_to_all(sides_flat, ('row', 'col'), split_axis=1, concat_axis=2, t...  53.2 us
    all_to_all x2, waiting for transfers between devices, to_tiles(): lax.all_to_all(arranged, ('row', 'col'), split_axis=1, concat_axis=0, til...  24.5 us
    slice x4, local copies, waits for them, and re-layouts, on_device(): full_sides[1]  13.3 us
    unnamed x2, other arithmetic  9.45 us
    all_to_all x2, starting transfers between devices, to_tiles(): lax.all_to_all(arranged, ('row', 'col'), split_axis=1, concat_axis=0, til...  9.19 us
    reshape x2, local copies, waits for them, and re-layouts, to_channels(): moved.reshape(stack_n, per_dev, rows_n, cols_n, tile_rows, tile_cols)  8.9 us
    another operation x4, local copies, waits for them, and re-layouts  8.23 us
    slice x2, local copies, waits for them, and re-layouts, on_device(): full_sides[0]  5.58 us
  transfers between devices with their start and end apart: 2, of which 2 were waited for; matrix products, arithmetic and copies ran while one was open for 2% of the time, Pallas kernels for 0%

commit v1 on v0

v1 whole, which is shorter than its diff:
```python
import functools

import jax
import jax.numpy as jnp
import numpy as np
from jax import lax
from jax.experimental import pallas as pl
from jax.experimental.pallas import tpu as pltpu
from jax.sharding import PartitionSpec as P

epsilon = 1e-05
F32 = jnp.float32
BF16 = jnp.bfloat16

BITS = ("y_hi", "y_lo", "z_lo", "x_hi", "x_lo", "z_hi", "core")
ORDER = BITS


def device_number(r, c):
    return 16 * r + c


def dot(a, b, dims):
    return lax.dot_general(a, b, (dims, ((), ())), preferred_element_type=F32)


def ahead(items, produce, consume):
    waiting = None
    for item in items:
        made = produce(item)
        if waiting is not None:
            consume(*waiting)
        waiting = (item, made)
    consume(*waiting)


def two_blocks(matrix):
    zero = jnp.zeros_like(matrix)
    return jnp.concatenate(
        [jnp.concatenate([matrix, zero], axis=1), jnp.concatenate([zero, matrix], axis=1)], axis=0
    )


def side_by_side(ref, n):
    return jnp.concatenate([ref[n : n + 512, :], ref[n + 512 : n + 1024, :]], axis=1)


def norm_rows(pair_ref, gain, centred_ref, normed_ref):
    row = lax.broadcasted_iota(jnp.int32, (128, 128), 0)
    column = lax.broadcasted_iota(jnp.int32, (128, 128), 1)
    centring = two_blocks(jnp.where(row == column, 127.0 / 128.0, -1.0 / 128.0).astype(BF16))
    average = two_blocks(jnp.full((128, 128), 1.0 / 128.0, BF16))
    gains = jnp.concatenate([gain, gain], axis=1)
    for n in range(0, 2048, 1024):
        centred_ref[n // 2 : n // 2 + 512, :] = dot(side_by_side(pair_ref, n), centring, ((1,), (0,)))

    def spread(n):
        centred = centred_ref[n // 2 : n // 2 + 512, :]
        return dot((centred * centred).astype(BF16), average, ((1,), (0,)))

    def scale(n, variance):
        normed = (centred_ref[n // 2 : n // 2 + 512, :] * lax.rsqrt(variance + epsilon) * gains).astype(BF16)
        normed_ref[n : n + 512, :] = normed[:, :128]
        normed_ref[n + 512 : n + 1024, :] = normed[:, 128:]

    ahead(range(0, 2048, 1024), spread, scale)


def swap_matrix():
    row = lax.broadcasted_iota(jnp.int32, (256, 256), 0)
    column = lax.broadcasted_iota(jnp.int32, (256, 256), 1)
    return jnp.where((row & 15) * 16 + (row >> 4) == column, 1.0, 0.0).astype(BF16)


def emit_sides(half_ref, swap, out_ref):
    def swapped(channel):
        return dot(swap, half_ref[:, channel : channel + 16, :].reshape(256, 256), ((1,), (0,))).astype(BF16)

    def store(channel, both):
        for side in range(2):
            part = both[:, 128 * side : 128 * side + 128].reshape(16, 16, 128)
            out_ref[channel : channel + 16, side] = part

    ahead(range(0, 128, 16), swapped, store)


def project(pair_ref, gain, wt_ref, gate_weight, swap, refs, out_ref, gate_ref, strided=False):
    centred_ref, normed_ref, half_ref = refs
    norm_rows(pair_ref, gain, centred_ref, normed_ref)
    slabs = normed_ref.reshape(4, 16, 32, 128)
    def product(place):
        s, side = place
        normed = jnp.concatenate([slabs[:, s + n].reshape(128, 128) for n in range(2)], axis=0)
        return dot(wt_ref[256 * side : 256 * side + 256], normed, ((1,), (1,))).reshape(16, 2, 8, 256)

    def gated(place, both):
        s, side = place
        result = (both[:, 0] + both[:, 0] * jnp.tanh(both[:, 1])).reshape(128, 256)
        for n in range(2):
            if strided:
                half_ref[pl.ds(side * 16 + s + n, 128, stride=40), :] = result[:, 128 * n : 128 * n + 128]
                continue
            result = result.astype(BF16)
            half_ref[s + n, :, 128 * side : 128 * side + 128] = result[:, 128 * n : 128 * n + 128]

    ahead([(s, side) for s in range(0, 16, 2) for side in range(2)], product, gated)
    weight = two_blocks(halved(gate_weight))

    def gate_product(n):
        return dot(side_by_side(normed_ref, n), weight, ((1,), (0,)))

    def gate(n, values):
        values = jnp.tanh(values)
        gate_ref[n : n + 512, :] = values[:, :128]
        gate_ref[n + 512 : n + 1024, :] = values[:, 128:]

    ahead(range(0, 2048, 1024), gate_product, gate)
    if strided:
        for channel in range(0, 128, 16):
            part = half_ref[channel * 40 : channel * 40 + 640, :].reshape(16, 40, 128)[:, :32]
            out_ref[channel : channel + 16] = part.astype(BF16).reshape(16, 2, 16, 128)
    else:
        emit_sides(half_ref, swap, out_ref)


def halved(weight):
    return (0.5 * weight.astype(F32)).astype(BF16)


def fill_weights(side_ref, wt_ref, update):
    for side in range(2):
        value, gate = [
            (0.5 * side_ref[4 * update + 2 * side + n].astype(F32)).T.reshape(16, 1, 8, 128) for n in range(2)
        ]
        both = jnp.concatenate([value, gate], axis=1).reshape(256, 128)
        wt_ref[256 * side : 256 * side + 256, :] = both.astype(BF16)


def project_kernel(
    pair_hbm, side_hbm, gate_weight_hbm, gain_hbm, out_gain_hbm, out_ref, gate_ref, gain_ref, pair_ref, side_ref, gate_weight_ref,
    wt_ref, centred_ref, normed_ref, half_ref, sems,
):
    copies = [
        pltpu.make_async_copy(side_hbm.at[pl.ds(0, 4)], side_ref, sems.at[0]),
        pltpu.make_async_copy(pair_hbm, pair_ref, sems.at[1]),
        pltpu.make_async_copy(gate_weight_hbm.at[0], gate_weight_ref, sems.at[2]),
        pltpu.make_async_copy(gain_hbm, gain_ref.at[0], sems.at[3]),
        pltpu.make_async_copy(out_gain_hbm, gain_ref.at[1], sems.at[4]),
    ]
    for copy in copies:
        copy.start()
    copies[0].wait()
    fill_weights(side_ref, wt_ref, 0)
    for copy in copies[1:]:
        copy.wait()
    project(
        pair_ref, gain_ref[0, 0:1, :], wt_ref, gate_weight_ref[...], None,
        (centred_ref, normed_ref, half_ref), out_ref, gate_ref, True,
    )


def swap_groups(groups, low, even):
    halves = [pair for t in groups for pair in ((t[0], t[2]), (t[1], t[3]))]
    moved = [pltpu.roll(jnp.where(low, b, a), 64, 1) for a, b in halves]
    halves = [(jnp.where(low, a, m), jnp.where(low, m, b)) for (a, b), m in zip(halves, moved)]
    crossed = []
    for (u0, u2), (u1, u3) in zip(halves[::2], halves[1::2]):
        crossed += [(u0, u1), (u2, u3)]
    rolled = [(pltpu.roll(b, 32, 1), pltpu.roll(a, 96, 1)) for a, b in crossed]
    out = [
        (jnp.where(even, a, to_first), jnp.where(even, to_second, b))
        for (a, b), (to_first, to_second) in zip(crossed, rolled)
    ]
    return [first + second for first, second in zip(out[::2], out[1::2])]


def triangle_kernel(in_ref, regroup_ref, out_ref, left_ref, right_ref, *, update):
    lane = lax.broadcasted_iota(jnp.int32, (16, 128), 1)
    low = lane < 64
    even = (lane & 32) == 0


    def stacked(side, places):
        tiles = []
        for n in range(4):
            numbers = [device_number(r, 4 * block + n) for r, block in places]
            tiles.append(jnp.concatenate([in_ref[32 * m + 16 * side : 32 * m + 16 * side + 16, :] for m in numbers], axis=0))
        return jnp.concatenate(tiles, axis=1)

    for half in range(2):
        if update == 0:
            places = [(4 * half + r, block) for r in range(4) for block in range(4)]
            regrouped = dot(stacked(1, places), regroup_ref[...], ((1,), (0,))).astype(BF16)
            for m, (r, block) in enumerate(places):
                for g in range(4):
                    row = r * 64 + g * 16
                    tile = regrouped[16 * m : 16 * m + 16, 128 * g : 128 * g + 128]
                    right_ref[row : row + 16, 128 * block : 128 * block + 128] = tile
        else:
            places = [(r, 2 * half + block) for block in range(2) for r in range(8)]
            regrouped = dot(regroup_ref[...], stacked(0, places), ((1,), (1,))).astype(BF16)
            for block in range(2):
                for g in range(4):
                    row = 128 * (2 * half + block)
                    tile = regrouped[128 * g : 128 * g + 128, 128 * block : 128 * block + 128]
                    left_ref[row : row + 128, 128 * g : 128 * g + 128] = tile
    side, full_ref = ((0, left_ref), (1, right_ref))[update]
    places = [(r, block) for r in range(8) for block in range(4)]
    groups = []
    for r, block in places:
        numbers = [device_number(r, 4 * block + n) for n in range(4)]
        groups.append([in_ref[32 * m + 16 * side : 32 * m + 16 * side + 16, :] for m in numbers])
    for (r, block), tiles in zip(places, swap_groups(groups, low, even)):
        for g, tile in enumerate(tiles):
            row = r * 64 + g * 16 if update == 0 else g * 128 + r * 16
            full_ref[row : row + 16, 128 * block : 128 * block + 128] = tile
    products = []
    for half in range(2):
        part = slice(256 * half, 256 * half + 256)
        if update == 0:
            products.append(dot(left_ref[...], right_ref[part, :], ((1,), (1,))).astype(BF16))
        else:
            products.append(dot(left_ref[...], right_ref[:, part], ((1,), (0,))).astype(BF16))
    for half, mixed in enumerate(products):
        places = [(r, block) for r in range(8) for block in range(2)]
        groups = [
            [mixed[r * 64 + 16 * g : r * 64 + 16 * g + 16, 128 * block : 128 * block + 128] for g in range(4)]
            for r, block in places
        ]
        for (r, block), tiles in zip(places, swap_groups(groups, low, even)):
            for n, tile in enumerate(tiles):
                row = device_number(r, 8 * half + 4 * block + n) * 16
                out_ref[row : row + 16, :] = tile


def finish_kernel(mixed_ref, pair_ref, gate_ref, out_weight_ref, gain_ref, *rest, update):
    if update == 0:
        (side_ref, gate_weight_ref, pair_out_ref, out_ref, gate_out_ref, raw_ref, wt_ref, centred_ref,
         normed_ref, half_ref) = rest
    else:
        pair_hbm, raw_ref, pair_out_ref, sems = rest
    if update == 0:
        fill_weights(side_ref, wt_ref, 1)
    swap = swap_matrix()

    def swapped(row):
        pieces = [mixed_ref[row + 256 * n : row + 256 * n + 256, :] for n in range(2)]
        return dot(swap, jnp.concatenate(pieces, axis=1), ((1,), (0,)))

    def store(row, both):
        for n in range(2):
            channel = row // 16 + 16 * n
            raw_ref[:, channel : channel + 16, :] = both[:, 128 * n : 128 * n + 128].reshape(16, 16, 128)

    ahead(range(0, 2048, 512), swapped, store)
    out_gain = jnp.broadcast_to(gain_ref[1, update : update + 1, :], (128, 128)).T
    weight = two_blocks(halved(out_weight_ref[update]))
    slabs = [ref.reshape(4, 16, 32, 128) for ref in (pair_ref, gate_ref, pair_out_ref)]
    copies = []
    out_normed = {}
    for s in range(0, 18, 2):
        if s < 16:
            values = raw_ref[s : s + 2]
            centred = values - jnp.mean(values, axis=1, keepdims=True)
            variance = jnp.mean(centred * centred, axis=1, keepdims=True)
            out_normed[s] = (centred * lax.rsqrt(variance + epsilon) * out_gain).astype(BF16)
        if s == 0:
            continue
        changes = dot(out_normed[s - 2].reshape(256, 128), weight, ((0,), (0,)))
        for n in range(2):
            change = changes[:, 128 * n : 128 * n + 128].reshape(4, 32, 128)
            before, gate = slabs[0][:, s - 2 + n].astype(F32), slabs[1][:, s - 2 + n]
            slabs[2][:, s - 2 + n] = (before + (change + change * gate)).astype(BF16)
        if update == 1 and s % 4 == 0:
            part = pl.ds(s - 4, 4)
            copies.append(pltpu.make_async_copy(slabs[2].at[:, part], pair_hbm.at[:, part], sems.at[s // 4 - 1]))
            copies[-1].start()
    for copy in copies:
        copy.wait()
    if update == 0:
        project(
            pair_out_ref, gain_ref[0, 1:2, :], wt_ref, gate_weight_ref[1], swap,
            (centred_ref, normed_ref, half_ref), out_ref, gate_out_ref,
        )


def call(kernel, out, scratch, *operands, hbm=(), hbm_out=False):
    operands = [pltpu.with_memory_space_constraint(a, pltpu.HBM) if n in hbm else a for n, a in enumerate(operands)]
    spaces = [pltpu.HBM if n in hbm else pltpu.VMEM for n in range(len(operands))]
    return pl.pallas_call(
        kernel,
        out_shape=[jax.ShapeDtypeStruct(*one) for one in out],
        in_specs=[pl.BlockSpec(memory_space=space) for space in spaces],
        out_specs=[pl.BlockSpec(memory_space=pltpu.HBM if hbm_out else pltpu.VMEM) for _ in out],
        scratch_shapes=[pltpu.VMEM(*one) if isinstance(one, tuple) else one for one in scratch],
        compiler_params=pltpu.CompilerParams(vmem_limit_bytes=32 * 1024 * 1024),
    )(*operands)


SIDES = ((128, 2, 16, 128), BF16)
MIXED = ((2048, 128), BF16)
PAIR = ((2048, 128), BF16)
GATE = ((2048, 128), F32)
GAIN = ((2, 2, 128), F32)
PROJECT_SCRATCH = [((512, 128), BF16), ((1024, 256), F32), ((2048, 128), BF16), ((16, 128, 256), BF16)]


def exchange(flat):
    pieces = flat.reshape(128, -1, 128)
    moved = lax.all_to_all(pieces, ORDER, split_axis=0, concat_axis=0, tiled=True)
    return moved.reshape(-1, 128)


def on_device(pair_rep, side_weight, gate_weight, out_weight, in_gain, out_gain):
    pair = pair_rep.reshape(PAIR[0])
    side_weight = side_weight.reshape(8, 128, 128)
    sides, gate, gains = call(
        project_kernel,
        [SIDES, GATE, GAIN],
        [PAIR, ((4, 128, 128), BF16), ((128, 128), BF16), *PROJECT_SCRATCH[:-1], ((5120, 128), F32), pltpu.SemaphoreType.DMA((5,))],
        pair, side_weight, gate_weight, in_gain, out_gain,
        hbm=range(5),
    )
    regroup = jnp.asarray(np.eye(512).reshape(4, 4, 32, 512).transpose(1, 0, 2, 3).reshape(512, 512).T, BF16)
    finish_scratch = [((16, 128, 128), F32)]
    for update in range(2):
        sides = exchange(sides)
        triangle = functools.partial(triangle_kernel, update=update)
        (mixed,) = call(triangle, [MIXED], [((512, 512), BF16)] * 2, sides, regroup)
        mixed = exchange(mixed)
        finish = functools.partial(finish_kernel, update=update)
        operands = (mixed, pair, gate, out_weight, gains)
        if update == 0:
            pair, sides, gate = call(
                finish, [PAIR, SIDES, GATE], finish_scratch + PROJECT_SCRATCH,
                *operands, side_weight, gate_weight,
            )
        else:
            scratch = finish_scratch + [PAIR, pltpu.SemaphoreType.DMA((4,))]
            (pair,) = call(finish, [((4, 16, 32, 128), BF16)], scratch, *operands, hbm_out=True)
    return pair.reshape(pair_rep.shape)


def solution(mesh):
    physical = jax.sharding.Mesh(mesh.devices.reshape((2,) * 7), BITS)
    tile = P(BITS[:3], BITS[3:], None)
    return jax.shard_map(
        on_device, mesh=physical, in_specs=(tile, P(), P(), P(), P(), P()), out_specs=tile, check_vma=False
    )
```

time: 171 us -> 97.1 us (0.57)
  local copies, waits for them, and re-layouts: 56.6 us -> 0.03 us
  blocking collectives: 53.2 us -> 88.6 us
  waiting for transfers between devices: 24.5 us -> 0 us
  other arithmetic: 17.1 us -> 0 us
  matrix products: 9.65 us -> 0 us
  starting transfers between devices: 9.19 us -> 0 us
  Pallas kernels: 0 us -> 8.12 us
    all_to_all x2 -> x4, blocking collectives: 53.2 us -> 88.6 us  [exchange(): lax.all_to_all(pieces, ORDER, split_axis=0, concat_axis=0, tiled=True)]
    all_to_all x2 -> x0, waiting for transfers between devices: 24.5 us -> none  [to_tiles(): lax.all_to_all(arranged, ('row', 'col'), split_axis=1, concat_axis=0, til...]
    slice x7 -> x0, local copies, waits for them, and re-layouts: 18.9 us -> none  [the longest x4 13.3 us: on_device(): full_sides[1]]
    reshape x4 -> x0, local copies, waits for them, and re-layouts: 12 us -> none  [the longest x2 8.9 us: to_channels(): moved.reshape(stack_n, per_dev, rows_n, cols_n, tile_rows, tile_cols)]
    another operation x6 -> x0, local copies, waits for them, and re-layouts: 10.2 us -> none
    dot_general x14 -> x0, matrix products: 9.65 us -> none  [the longest x2 2.83 us: on_device(): jnp.dot(normed, gate_weight[update], preferred_element_type=jnp.float32)]
    unnamed x2 -> x0, other arithmetic: 9.45 us -> none
    all_to_all x2 -> x0, starting transfers between devices: 9.19 us -> none  [to_tiles(): lax.all_to_all(arranged, ('row', 'col'), split_axis=1, concat_axis=0, til...]
  transfers between devices with their start and end apart: 2 -> 0, of which waited for: 2 -> 0; matrix products, arithmetic and copies ran while one was open for 2% -> 0% of each run, Pallas kernels for 0% -> 0%
where the time goes in v1:
time: 97.1 us; the launch traced here: 96.9 us
  blocking collectives  88.6 us (91%)
  Pallas kernels  8.12 us (8%)
    all_to_all x4, blocking collectives, exchange(): lax.all_to_all(pieces, ORDER, split_axis=0, concat_axis=0, tiled=True)  88.6 us
    pallas_call x5, Pallas kernels, call(): pl.pallas_call(kernel, out_shape=[jax.ShapeDtypeStruct(*one) for one in o...  8.12 us

profile of v1, /device:TPU:1, one launch (start us, length us, event | category | flops | bytes accessed | tf_op | source)
XLA Modules:
  0.0 96.9 jit_solution(12915514222512788908)
XLA Ops:
  0.0 2.4 %shard_map.73 = (bf16[128,2,16,128]{3,2,1,0:T(8,128)(2,1)S(1)}, f32[2048,128]{1,0:T(8,128)S(1)}, f32[2,2,128]{2,1,0:T(2,128)S(1)}) custom-call(bf16[2048,128]{1,0:T(8,128)(2,1)} %bitcast.17, bf16[8,128,128]{2,1,0:T(8,128)(2,1)} %bitcast.21, bf16[2,128,128]{2,1,0:T(8,128)(2,1)} %rest_1_.1, f32[2,128]{1,0:T(2,128)} %gain_hbm.1, f32[2,128]{1,0:T(2,128)} %out_gain_hbm.1), custom_call_target="tpu_custom_call" | custom-call | tf_op jit(solution)/shard_map/pallas_call | solution.py:290
  2.4 0.0 copy-start.1
  2.5 30.2 %all_to_all.20 = bf16[128,32,128]{2,1,0:T(8,128)(2,1)S(1)} all-to-all(bf16[128,32,128]{2,1,0:T(8,128)(2,1)S(1)} %bitcast.20), channel_id=1, replica_groups=mesh['y_hi'=2,'y_lo'=2,'z_lo'=2,'x_hi'=2,'x_lo'=2,'z_hi'=2,'core'=2] {'y..., dimensions={0} | all-to-all | bytes 2097152 | tf_op jit(solution)/shard_map/all_to_all | solution.py:310
  32.7 0.0 copy-done.1
  32.7 1.1 %shard_map.74 = bf16[2048,128]{1,0:T(8,128)(2,1)S(1)} custom-call(bf16[4096,128]{1,0:T(8,128)(2,1)S(1)} %bitcast.12, bf16[512,512]{1,0:T(8,128)(2,1)S(1)} %copy-done.1), custom_call_target="tpu_custom_call" | custom-call | tf_op jit(solution)/shard_map/pallas_call | solution.py:290
  33.8 0.0 copy-start
  33.8 0.0 copy-start.2
  33.8 0.0 copy-start.3
  33.8 0.0 copy-start.4
  33.8 17.8 %all_to_all.21 = bf16[128,16,128]{2,1,0:T(8,128)(2,1)S(1)} all-to-all(bf16[128,16,128]{2,1,0:T(8,128)(2,1)S(1)} %bitcast.16), channel_id=1, replica_groups=mesh['y_hi'=2,'y_lo'=2,'z_lo'=2,'x_hi'=2,'x_lo'=2,'z_hi'=2,'core'=2] {'y..., dimensions={0} | all-to-all | bytes 1048576 | tf_op jit(solution)/shard_map/all_to_all | solution.py:310
  51.6 0.0 copy-done
  51.6 0.0 copy-done.2
  51.6 0.0 copy-done.3
  51.6 0.0 copy-done.4
  51.6 2.1 %shard_map.75 = (bf16[2048,128]{1,0:T(8,128)(2,1)S(1)}, bf16[128,2,16,128]{3,2,1,0:T(8,128)(2,1)S(1)}, f32[2048,128]{1,0:T(8,128)S(1)}) custom-call(bf16[2048,128]{1,0:T(8,128)(2,1)S(1)} %bitcast.13, bf16[2048,128]{1,0:T(8,128)(2,1)S(1)} %bitcast.18, f32[2048,128]{1,0:T(8,128)S(1)} %get-tuple-element.12.gate_ref, bf16[2,128,128]{2,1,0:T(8,128)(2,1)S(1)} %copy-done.3, ...), custom_call_target="tpu_custom_call" | custom-call | tf_op jit(solution)/shard_map/pallas_call | solution.py:290
  53.7 23.0 %all_to_all.22 = bf16[128,32,128]{2,1,0:T(8,128)(2,1)S(1)} all-to-all(bf16[128,32,128]{2,1,0:T(8,128)(2,1)S(1)} %bitcast.19), channel_id=1, replica_groups=mesh['y_hi'=2,'y_lo'=2,'z_lo'=2,'x_hi'=2,'x_lo'=2,'z_hi'=2,'core'=2] {'y..., dimensions={0} | all-to-all | bytes 2097152 | tf_op jit(solution)/shard_map/all_to_all | solution.py:310
  76.7 1.0 %shard_map.76 = bf16[2048,128]{1,0:T(8,128)(2,1)S(1)} custom-call(bf16[4096,128]{1,0:T(8,128)(2,1)S(1)} %bitcast.11, bf16[512,512]{1,0:T(8,128)(2,1)S(1)} %copy-done.1), custom_call_target="tpu_custom_call" | custom-call | tf_op jit(solution)/shard_map/pallas_call | solution.py:290
  77.8 17.6 %all_to_all.23 = bf16[128,16,128]{2,1,0:T(8,128)(2,1)S(1)} all-to-all(bf16[128,16,128]{2,1,0:T(8,128)(2,1)S(1)} %bitcast.15), channel_id=1, replica_groups=mesh['y_hi'=2,'y_lo'=2,'z_lo'=2,'x_hi'=2,'x_lo'=2,'z_hi'=2,'core'=2] {'y..., dimensions={0} | all-to-all | bytes 1048576 | tf_op jit(solution)/shard_map/all_to_all | solution.py:310
  95.4 1.5 %shard_map.77 = bf16[4,16,32,128]{3,2,1,0:T(8,128)(2,1)} custom-call(bf16[2048,128]{1,0:T(8,128)(2,1)S(1)} %bitcast.14, bf16[2048,128]{1,0:T(8,128)(2,1)S(1)} %get-tuple-element.15.pair_ref, f32[2048,128]{1,0:T(8,128)S(1)} %get-tuple-element.16.gate_ref, bf16[2,128,128]{2,1,0:T(8,128)(2,1)S(1)} %copy-done.3, f32[2,2,128]{2,1,0:T(2,128)S(1)} %get-tuple-element.13.gain_ref), custom_call_target="tpu_custom_call" | custom-call | tf_op jit(solution)/shard_map/pallas_call | solution.py:290
Async XLA Ops:
  2.4 30.3 %copy-start.1 = (bf16[512,512]{1,0:T(8,128)(2,1)S(1)}, bf16[512,512]{1,0:T(8,128)(2,1)}, u32[]{:S(2)}) copy-start(bf16[512,512]{1,0:T(8,128)(2,1)} %constant.2.clone.regroup_ref) | copy-start | bytes 1572868
  33.8 17.8 %copy-start = (bf16[64,32,128]{2,1,0:T(8,128)(2,1)S(1)}, bf16[64,32,128]{2,1,0:T(8,128)(2,1)}, u32[]{:S(2)}) copy-start(bf16[64,32,128]{2,1,0:T(8,128)(2,1)} %param.7) | copy-start | bytes 1572868
  33.8 17.8 %copy-start.2 = (bf16[2,2,2,128,128]{4,3,2,1,0:T(8,128)(2,1)S(1)}, bf16[2,2,2,128,128]{4,3,2,1,0:T(8,128)(2,1)}, u32[]{:S(2)}) copy-start(bf16[2,2,2,128,128]{4,3,2,1,0:T(8,128)(2,1)} %param.8) | copy-start | bytes 786436
  33.8 17.8 %copy-start.3 = (bf16[2,128,128]{2,1,0:T(8,128)(2,1)S(1)}, bf16[2,128,128]{2,1,0:T(8,128)(2,1)}, u32[]{:S(2)}) copy-start(bf16[2,128,128]{2,1,0:T(8,128)(2,1)} %out_weight_ref.3) | copy-start | bytes 196612
  33.8 17.8 %copy-start.4 = (bf16[2,128,128]{2,1,0:T(8,128)(2,1)S(1)}, bf16[2,128,128]{2,1,0:T(8,128)(2,1)}, u32[]{:S(2)}) copy-start(bf16[2,128,128]{2,1,0:T(8,128)(2,1)} %rest_1_.1) | copy-start | bytes 196612

commit v2 on v1

--- a/solution.py
+++ b/solution.py
@@ -72,19 +72,7 @@
     return jnp.where((row & 15) * 16 + (row >> 4) == column, 1.0, 0.0).astype(BF16)
 
 
-def emit_sides(half_ref, swap, out_ref):
-    def swapped(channel):
-        return dot(swap, half_ref[:, channel : channel + 16, :].reshape(256, 256), ((1,), (0,))).astype(BF16)
-
-    def store(channel, both):
-        for side in range(2):
-            part = both[:, 128 * side : 128 * side + 128].reshape(16, 16, 128)
-            out_ref[channel : channel + 16, side] = part
-
-    ahead(range(0, 128, 16), swapped, store)
-
-
-def project(pair_ref, gain, wt_ref, gate_weight, swap, refs, out_ref, gate_ref, strided=False):
+def project(pair_ref, gain, wt_ref, gate_weight, refs, out_ref, gate_ref):
     centred_ref, normed_ref, half_ref = refs
     norm_rows(pair_ref, gain, centred_ref, normed_ref)
     slabs = normed_ref.reshape(4, 16, 32, 128)
@@ -97,11 +85,7 @@
         s, side = place
         result = (both[:, 0] + both[:, 0] * jnp.tanh(both[:, 1])).reshape(128, 256)
         for n in range(2):
-            if strided:
-                half_ref[pl.ds(side * 16 + s + n, 128, stride=40), :] = result[:, 128 * n : 128 * n + 128]
-                continue
-            result = result.astype(BF16)
-            half_ref[s + n, :, 128 * side : 128 * side + 128] = result[:, 128 * n : 128 * n + 128]
+            half_ref[pl.ds(side * 16 + s + n, 128, stride=40), :] = result[:, 128 * n : 128 * n + 128]
 
     ahead([(s, side) for s in range(0, 16, 2) for side in range(2)], product, gated)
     weight = two_blocks(halved(gate_weight))
@@ -115,12 +99,9 @@
         gate_ref[n + 512 : n + 1024, :] = values[:, 128:]
 
     ahead(range(0, 2048, 1024), gate_product, gate)
-    if strided:
-        for channel in range(0, 128, 16):
-            part = half_ref[channel * 40 : channel * 40 + 640, :].reshape(16, 40, 128)[:, :32]
-            out_ref[channel : channel + 16] = part.astype(BF16).reshape(16, 2, 16, 128)
-    else:
-        emit_sides(half_ref, swap, out_ref)
+    for channel in range(0, 128, 16):
+        part = half_ref[channel * 40 : channel * 40 + 640, :].reshape(16, 40, 128)[:, :32]
+        out_ref[channel : channel + 16] = part.astype(BF16).reshape(16, 2, 16, 128)
 
 
 def halved(weight):
@@ -154,8 +135,8 @@
     for copy in copies[1:]:
         copy.wait()
     project(
-        pair_ref, gain_ref[0, 0:1, :], wt_ref, gate_weight_ref[...], None,
-        (centred_ref, normed_ref, half_ref), out_ref, gate_ref, True,
+        pair_ref, gain_ref[0, 0:1, :], wt_ref, gate_weight_ref[...],
+        (centred_ref, normed_ref, half_ref), out_ref, gate_ref,
     )
 
 
@@ -241,18 +222,24 @@
         pair_hbm, raw_ref, pair_out_ref, sems = rest
     if update == 0:
         fill_weights(side_ref, wt_ref, 1)
-    swap = swap_matrix()
-
-    def swapped(row):
-        pieces = [mixed_ref[row + 256 * n : row + 256 * n + 256, :] for n in range(2)]
-        return dot(swap, jnp.concatenate(pieces, axis=1), ((1,), (0,)))
-
-    def store(row, both):
-        for n in range(2):
-            channel = row // 16 + 16 * n
-            raw_ref[:, channel : channel + 16, :] = both[:, 128 * n : 128 * n + 128].reshape(16, 16, 128)
-
-    ahead(range(0, 2048, 512), swapped, store)
+    if update == 0:
+        swap = swap_matrix()
+
+        def swapped(row):
+            pieces = [mixed_ref[row + 256 * n : row + 256 * n + 256, :] for n in range(2)]
+            return dot(swap, jnp.concatenate(pieces, axis=1), ((1,), (0,)))
+
+        def store(row, both):
+            for n in range(2):
+                channel = row // 16 + 16 * n
+                raw_ref[:, channel : channel + 16, :] = both[:, 128 * n : 128 * n + 128].reshape(16, 16, 128)
+
+        ahead(range(0, 2048, 512), swapped, store)
+    else:
+        for channel in range(0, 128, 16):
+            part = mixed_ref[16 * channel : 16 * channel + 256, :].astype(F32).reshape(16, 16, 128)
+            for n in range(16):
+                raw_ref[24 * (channel + n) : 24 * (channel + n) + 16, :] = part[n]
     out_gain = jnp.broadcast_to(gain_ref[1, update : update + 1, :], (128, 128)).T
     weight = two_blocks(halved(out_weight_ref[update]))
     slabs = [ref.reshape(4, 16, 32, 128) for ref in (pair_ref, gate_ref, pair_out_ref)]
@@ -260,7 +247,10 @@
     out_normed = {}
     for s in range(0, 18, 2):
         if s < 16:
-            values = raw_ref[s : s + 2]
+            if update == 0:
+                values = raw_ref[s : s + 2]
+            else:
+                values = jnp.stack([raw_ref[pl.ds(s + n, 128, stride=24), :] for n in range(2)])
             centred = values - jnp.mean(values, axis=1, keepdims=True)
             variance = jnp.mean(centred * centred, axis=1, keepdims=True)
             out_normed[s] = (centred * lax.rsqrt(variance + epsilon) * out_gain).astype(BF16)
@@ -279,7 +269,7 @@
         copy.wait()
     if update == 0:
         project(
-            pair_out_ref, gain_ref[0, 1:2, :], wt_ref, gate_weight_ref[1], swap,
+            pair_out_ref, gain_ref[0, 1:2, :], wt_ref, gate_weight_ref[1],
             (centred_ref, normed_ref, half_ref), out_ref, gate_out_ref,
         )
 
@@ -302,7 +292,7 @@
 PAIR = ((2048, 128), BF16)
 GATE = ((2048, 128), F32)
 GAIN = ((2, 2, 128), F32)
-PROJECT_SCRATCH = [((512, 128), BF16), ((1024, 256), F32), ((2048, 128), BF16), ((16, 128, 256), BF16)]
+PROJECT_SCRATCH = [((512, 128), BF16), ((1024, 256), F32), ((2048, 128), BF16), ((5120, 128), F32)]
 
 
 def exchange(flat):
@@ -317,7 +307,7 @@
     sides, gate, gains = call(
         project_kernel,
         [SIDES, GATE, GAIN],
-        [PAIR, ((4, 128, 128), BF16), ((128, 128), BF16), *PROJECT_SCRATCH[:-1], ((5120, 128), F32), pltpu.SemaphoreType.DMA((5,))],
+        [PAIR, ((4, 128, 128), BF16), ((128, 128), BF16), *PROJECT_SCRATCH, pltpu.SemaphoreType.DMA((5,))],
         pair, side_weight, gate_weight, in_gain, out_gain,
         hbm=range(5),
     )
@@ -336,7 +326,7 @@
                 *operands, side_weight, gate_weight,
             )
         else:
-            scratch = finish_scratch + [PAIR, pltpu.SemaphoreType.DMA((4,))]
+            scratch = [((3072, 128), F32), PAIR, pltpu.SemaphoreType.DMA((4,))]
             (pair,) = call(finish, [((4, 16, 32, 128), BF16)], scratch, *operands, hbm_out=True)
     return pair.reshape(pair_rep.shape)
 

time: 97.1 us -> 96.8 us (level)
  no operation moved by 1% of the time
where the time goes in v2:
time: 96.8 us; the launch traced here: 96.6 us
  blocking collectives  88.6 us (92%)
  Pallas kernels  7.84 us (8%)
    all_to_all x4, blocking collectives, exchange(): lax.all_to_all(pieces, ORDER, split_axis=0, concat_axis=0, tiled=True)  88.6 us
    pallas_call x5, Pallas kernels, call(): pl.pallas_call(kernel, out_shape=[jax.ShapeDtypeStruct(*one) for one in o...  7.84 us

profile of v2, /device:TPU:1, one launch (start us, length us, event | category | flops | bytes accessed | tf_op | source)
XLA Modules:
  0.0 96.6 jit_solution(17656799778800033845)
XLA Ops:
  0.0 2.4 %shard_map.73 = (bf16[128,2,16,128]{3,2,1,0:T(8,128)(2,1)S(1)}, f32[2048,128]{1,0:T(8,128)S(1)}, f32[2,2,128]{2,1,0:T(2,128)S(1)}) custom-call(bf16[2048,128]{1,0:T(8,128)(2,1)} %bitcast.17, bf16[8,128,128]{2,1,0:T(8,128)(2,1)} %bitcast.21, bf16[2,128,128]{2,1,0:T(8,128)(2,1)} %rest_1_.1, f32[2,128]{1,0:T(2,128)} %gain_hbm.1, f32[2,128]{1,0:T(2,128)} %out_gain_hbm.1), custom_call_target="tpu_custom_call" | custom-call | tf_op jit(solution)/shard_map/pallas_call | solution.py:280
  2.4 0.0 copy-start.1
  2.5 30.2 %all_to_all.20 = bf16[128,32,128]{2,1,0:T(8,128)(2,1)S(1)} all-to-all(bf16[128,32,128]{2,1,0:T(8,128)(2,1)S(1)} %bitcast.20), channel_id=1, replica_groups=mesh['y_hi'=2,'y_lo'=2,'z_lo'=2,'x_hi'=2,'x_lo'=2,'z_hi'=2,'core'=2] {'y..., dimensions={0} | all-to-all | bytes 2097152 | tf_op jit(solution)/shard_map/all_to_all | solution.py:300
  32.7 0.0 copy-done.1
  32.7 1.1 %shard_map.74 = bf16[2048,128]{1,0:T(8,128)(2,1)S(1)} custom-call(bf16[4096,128]{1,0:T(8,128)(2,1)S(1)} %bitcast.12, bf16[512,512]{1,0:T(8,128)(2,1)S(1)} %copy-done.1), custom_call_target="tpu_custom_call" | custom-call | tf_op jit(solution)/shard_map/pallas_call | solution.py:280
  33.8 0.0 copy-start
  33.8 0.0 copy-start.2
  33.8 0.0 copy-start.3
  33.8 0.0 copy-start.4
  33.8 17.8 %all_to_all.21 = bf16[128,16,128]{2,1,0:T(8,128)(2,1)S(1)} all-to-all(bf16[128,16,128]{2,1,0:T(8,128)(2,1)S(1)} %bitcast.16), channel_id=1, replica_groups=mesh['y_hi'=2,'y_lo'=2,'z_lo'=2,'x_hi'=2,'x_lo'=2,'z_hi'=2,'core'=2] {'y..., dimensions={0} | all-to-all | bytes 1048576 | tf_op jit(solution)/shard_map/all_to_all | solution.py:300
  51.6 0.0 copy-done
  51.6 0.0 copy-done.2
  51.6 0.0 copy-done.3
  51.6 0.0 copy-done.4
  51.6 1.9 %shard_map.75 = (bf16[2048,128]{1,0:T(8,128)(2,1)S(1)}, bf16[128,2,16,128]{3,2,1,0:T(8,128)(2,1)S(1)}, f32[2048,128]{1,0:T(8,128)S(1)}) custom-call(bf16[2048,128]{1,0:T(8,128)(2,1)S(1)} %bitcast.13, bf16[2048,128]{1,0:T(8,128)(2,1)S(1)} %bitcast.18, f32[2048,128]{1,0:T(8,128)S(1)} %get-tuple-element.12.gate_ref, bf16[2,128,128]{2,1,0:T(8,128)(2,1)S(1)} %copy-done.3, ...), custom_call_target="tpu_custom_call" | custom-call | tf_op jit(solution)/shard_map/pallas_call | solution.py:280
  53.6 23.0 %all_to_all.22 = bf16[128,32,128]{2,1,0:T(8,128)(2,1)S(1)} all-to-all(bf16[128,32,128]{2,1,0:T(8,128)(2,1)S(1)} %bitcast.19), channel_id=1, replica_groups=mesh['y_hi'=2,'y_lo'=2,'z_lo'=2,'x_hi'=2,'x_lo'=2,'z_hi'=2,'core'=2] {'y..., dimensions={0} | all-to-all | bytes 2097152 | tf_op jit(solution)/shard_map/all_to_all | solution.py:300
  76.5 1.0 %shard_map.76 = bf16[2048,128]{1,0:T(8,128)(2,1)S(1)} custom-call(bf16[4096,128]{1,0:T(8,128)(2,1)S(1)} %bitcast.11, bf16[512,512]{1,0:T(8,128)(2,1)S(1)} %copy-done.1), custom_call_target="tpu_custom_call" | custom-call | tf_op jit(solution)/shard_map/pallas_call | solution.py:280
  77.6 17.6 %all_to_all.23 = bf16[128,16,128]{2,1,0:T(8,128)(2,1)S(1)} all-to-all(bf16[128,16,128]{2,1,0:T(8,128)(2,1)S(1)} %bitcast.15), channel_id=1, replica_groups=mesh['y_hi'=2,'y_lo'=2,'z_lo'=2,'x_hi'=2,'x_lo'=2,'z_hi'=2,'core'=2] {'y..., dimensions={0} | all-to-all | bytes 1048576 | tf_op jit(solution)/shard_map/all_to_all | solution.py:300
  95.2 1.4 %shard_map.77 = bf16[4,16,32,128]{3,2,1,0:T(8,128)(2,1)} custom-call(bf16[2048,128]{1,0:T(8,128)(2,1)S(1)} %bitcast.14, bf16[2048,128]{1,0:T(8,128)(2,1)S(1)} %get-tuple-element.15.pair_ref, f32[2048,128]{1,0:T(8,128)S(1)} %get-tuple-element.16.gate_ref, bf16[2,128,128]{2,1,0:T(8,128)(2,1)S(1)} %copy-done.3, f32[2,2,128]{2,1,0:T(2,128)S(1)} %get-tuple-element.13.gain_ref), custom_call_target="tpu_custom_call" | custom-call | tf_op jit(solution)/shard_map/pallas_call | solution.py:280
Async XLA Ops:
  2.4 30.3 %copy-start.1 = (bf16[512,512]{1,0:T(8,128)(2,1)S(1)}, bf16[512,512]{1,0:T(8,128)(2,1)}, u32[]{:S(2)}) copy-start(bf16[512,512]{1,0:T(8,128)(2,1)} %constant.2.clone.regroup_ref) | copy-start | bytes 1572868
  33.8 17.8 %copy-start = (bf16[64,32,128]{2,1,0:T(8,128)(2,1)S(1)}, bf16[64,32,128]{2,1,0:T(8,128)(2,1)}, u32[]{:S(2)}) copy-start(bf16[64,32,128]{2,1,0:T(8,128)(2,1)} %param.7) | copy-start | bytes 1572868
  33.8 17.8 %copy-start.2 = (bf16[2,2,2,128,128]{4,3,2,1,0:T(8,128)(2,1)S(1)}, bf16[2,2,2,128,128]{4,3,2,1,0:T(8,128)(2,1)}, u32[]{:S(2)}) copy-start(bf16[2,2,2,128,128]{4,3,2,1,0:T(8,128)(2,1)} %param.8) | copy-start | bytes 786436
  33.8 17.8 %copy-start.3 = (bf16[2,128,128]{2,1,0:T(8,128)(2,1)S(1)}, bf16[2,128,128]{2,1,0:T(8,128)(2,1)}, u32[]{:S(2)}) copy-start(bf16[2,128,128]{2,1,0:T(8,128)(2,1)} %out_weight_ref.3) | copy-start | bytes 196612
  33.8 17.8 %copy-start.4 = (bf16[2,128,128]{2,1,0:T(8,128)(2,1)S(1)}, bf16[2,128,128]{2,1,0:T(8,128)(2,1)}, u32[]{:S(2)}) copy-start(bf16[2,128,128]{2,1,0:T(8,128)(2,1)} %rest_1_.1) | copy-start | bytes 196612

commit v3 on v2

--- a/solution.py
+++ b/solution.py
@@ -45,14 +45,16 @@
     return jnp.concatenate([ref[n : n + 512, :], ref[n + 512 : n + 1024, :]], axis=1)
 
 
-def norm_rows(pair_ref, gain, centred_ref, normed_ref):
+def norm_rows(pair_ref, arrive, gain, centred_ref, normed_ref):
     row = lax.broadcasted_iota(jnp.int32, (128, 128), 0)
     column = lax.broadcasted_iota(jnp.int32, (128, 128), 1)
     centring = two_blocks(jnp.where(row == column, 127.0 / 128.0, -1.0 / 128.0).astype(BF16))
     average = two_blocks(jnp.full((128, 128), 1.0 / 128.0, BF16))
-    gains = jnp.concatenate([gain, gain], axis=1)
     for n in range(0, 2048, 1024):
+        arrive(n)
         centred_ref[n // 2 : n // 2 + 512, :] = dot(side_by_side(pair_ref, n), centring, ((1,), (0,)))
+
+    gains = jnp.concatenate([gain(), gain()], axis=1)
 
     def spread(n):
         centred = centred_ref[n // 2 : n // 2 + 512, :]
@@ -66,15 +68,9 @@
     ahead(range(0, 2048, 1024), spread, scale)
 
 
-def swap_matrix():
-    row = lax.broadcasted_iota(jnp.int32, (256, 256), 0)
-    column = lax.broadcasted_iota(jnp.int32, (256, 256), 1)
-    return jnp.where((row & 15) * 16 + (row >> 4) == column, 1.0, 0.0).astype(BF16)
-
-
-def project(pair_ref, gain, wt_ref, gate_weight, refs, out_ref, gate_ref):
+def project(pair_ref, arrive, gain, wt_ref, gate_weight, refs, out_ref, gate_ref):
     centred_ref, normed_ref, half_ref = refs
-    norm_rows(pair_ref, gain, centred_ref, normed_ref)
+    norm_rows(pair_ref, arrive, gain, centred_ref, normed_ref)
     slabs = normed_ref.reshape(4, 16, 32, 128)
     def product(place):
         s, side = place
@@ -88,7 +84,7 @@
             half_ref[pl.ds(side * 16 + s + n, 128, stride=40), :] = result[:, 128 * n : 128 * n + 128]
 
     ahead([(s, side) for s in range(0, 16, 2) for side in range(2)], product, gated)
-    weight = two_blocks(halved(gate_weight))
+    weight = two_blocks(halved(gate_weight()))
 
     def gate_product(n):
         return dot(side_by_side(normed_ref, n), weight, ((1,), (0,)))
@@ -121,21 +117,27 @@
     pair_hbm, side_hbm, gate_weight_hbm, gain_hbm, out_gain_hbm, out_ref, gate_ref, gain_ref, pair_ref, side_ref, gate_weight_ref,
     wt_ref, centred_ref, normed_ref, half_ref, sems,
 ):
+    halves = [pl.ds(n, 1024) for n in (0, 1024)]
     copies = [
-        pltpu.make_async_copy(side_hbm.at[pl.ds(0, 4)], side_ref, sems.at[0]),
-        pltpu.make_async_copy(pair_hbm, pair_ref, sems.at[1]),
-        pltpu.make_async_copy(gate_weight_hbm.at[0], gate_weight_ref, sems.at[2]),
-        pltpu.make_async_copy(gain_hbm, gain_ref.at[0], sems.at[3]),
-        pltpu.make_async_copy(out_gain_hbm, gain_ref.at[1], sems.at[4]),
+        *[pltpu.make_async_copy(pair_hbm.at[half], pair_ref.at[half], sems.at[n]) for n, half in enumerate(halves)],
+        pltpu.make_async_copy(side_hbm.at[pl.ds(0, 4)], side_ref, sems.at[2]),
+        pltpu.make_async_copy(gate_weight_hbm.at[0], gate_weight_ref, sems.at[3]),
+        pltpu.make_async_copy(gain_hbm, gain_ref.at[0], sems.at[4]),
+        pltpu.make_async_copy(out_gain_hbm, gain_ref.at[1], sems.at[5]),
     ]
     for copy in copies:
         copy.start()
-    copies[0].wait()
-    fill_weights(side_ref, wt_ref, 0)
-    for copy in copies[1:]:
-        copy.wait()
+
+    def arrive(n):
+        if n == 0:
+            copies[0].wait()
+        else:
+            for copy in copies[1:]:
+                copy.wait()
+            fill_weights(side_ref, wt_ref, 0)
+
     project(
-        pair_ref, gain_ref[0, 0:1, :], wt_ref, gate_weight_ref[...],
+        pair_ref, arrive, lambda: gain_ref[0, 0:1, :], wt_ref, lambda: gate_weight_ref[...],
         (centred_ref, normed_ref, half_ref), out_ref, gate_ref,
     )
 
@@ -222,24 +224,10 @@
         pair_hbm, raw_ref, pair_out_ref, sems = rest
     if update == 0:
         fill_weights(side_ref, wt_ref, 1)
-    if update == 0:
-        swap = swap_matrix()
-
-        def swapped(row):
-            pieces = [mixed_ref[row + 256 * n : row + 256 * n + 256, :] for n in range(2)]
-            return dot(swap, jnp.concatenate(pieces, axis=1), ((1,), (0,)))
-
-        def store(row, both):
-            for n in range(2):
-                channel = row // 16 + 16 * n
-                raw_ref[:, channel : channel + 16, :] = both[:, 128 * n : 128 * n + 128].reshape(16, 16, 128)
-
-        ahead(range(0, 2048, 512), swapped, store)
-    else:
-        for channel in range(0, 128, 16):
-            part = mixed_ref[16 * channel : 16 * channel + 256, :].astype(F32).reshape(16, 16, 128)
-            for n in range(16):
-                raw_ref[24 * (channel + n) : 24 * (channel + n) + 16, :] = part[n]
+    for channel in range(0, 128, 16):
+        part = mixed_ref[16 * channel : 16 * channel + 256, :].astype(F32).reshape(16, 16, 128)
+        for n in range(16):
+            raw_ref[24 * (channel + n) : 24 * (channel + n) + 16, :] = part[n]
     out_gain = jnp.broadcast_to(gain_ref[1, update : update + 1, :], (128, 128)).T
     weight = two_blocks(halved(out_weight_ref[update]))
     slabs = [ref.reshape(4, 16, 32, 128) for ref in (pair_ref, gate_ref, pair_out_ref)]
@@ -247,10 +235,7 @@
     out_normed = {}
     for s in range(0, 18, 2):
         if s < 16:
-            if update == 0:
-                values = raw_ref[s : s + 2]
-            else:
-                values = jnp.stack([raw_ref[pl.ds(s + n, 128, stride=24), :] for n in range(2)])
+            values = jnp.stack([raw_ref[pl.ds(s + n, 128, stride=24), :] for n in range(2)])
             centred = values - jnp.mean(values, axis=1, keepdims=True)
             variance = jnp.mean(centred * centred, axis=1, keepdims=True)
             out_normed[s] = (centred * lax.rsqrt(variance + epsilon) * out_gain).astype(BF16)
@@ -269,7 +254,7 @@
         copy.wait()
     if update == 0:
         project(
-            pair_out_ref, gain_ref[0, 1:2, :], wt_ref, gate_weight_ref[1],
+            pair_out_ref, lambda n: None, lambda: gain_ref[0, 1:2, :], wt_ref, lambda: gate_weight_ref[1],
             (centred_ref, normed_ref, half_ref), out_ref, gate_out_ref,
         )
 
@@ -307,12 +292,12 @@
     sides, gate, gains = call(
         project_kernel,
         [SIDES, GATE, GAIN],
-        [PAIR, ((4, 128, 128), BF16), ((128, 128), BF16), *PROJECT_SCRATCH, pltpu.SemaphoreType.DMA((5,))],
+        [PAIR, ((4, 128, 128), BF16), ((128, 128), BF16), *PROJECT_SCRATCH, pltpu.SemaphoreType.DMA((6,))],
         pair, side_weight, gate_weight, in_gain, out_gain,
         hbm=range(5),
     )
     regroup = jnp.asarray(np.eye(512).reshape(4, 4, 32, 512).transpose(1, 0, 2, 3).reshape(512, 512).T, BF16)
-    finish_scratch = [((16, 128, 128), F32)]
+    finish_scratch = [((3072, 128), F32)]
     for update in range(2):
         sides = exchange(sides)
         triangle = functools.partial(triangle_kernel, update=update)
@@ -326,7 +311,7 @@
                 *operands, side_weight, gate_weight,
             )
         else:
-            scratch = [((3072, 128), F32), PAIR, pltpu.SemaphoreType.DMA((4,))]
+            scratch = finish_scratch + [PAIR, pltpu.SemaphoreType.DMA((4,))]
             (pair,) = call(finish, [((4, 16, 32, 128), BF16)], scratch, *operands, hbm_out=True)
     return pair.reshape(pair_rep.shape)
 

time: 96.8 us -> 96.8 us (level)
  no operation moved by 1% of the time
where the time goes in v3:
time: 96.8 us; the launch traced here: 96.6 us
  blocking collectives  88.6 us (92%)
  Pallas kernels  7.83 us (8%)
    all_to_all x4, blocking collectives, exchange(): lax.all_to_all(pieces, ORDER, split_axis=0, concat_axis=0, tiled=True)  88.6 us
    pallas_call x5, Pallas kernels, call(): pl.pallas_call(kernel, out_shape=[jax.ShapeDtypeStruct(*one) for one in o...  7.83 us

profile of v3, /device:TPU:1, one launch (start us, length us, event | category | flops | bytes accessed | tf_op | source)
XLA Modules:
  0.0 96.6 jit_solution(16626227019070777399)
XLA Ops:
  0.0 2.5 %shard_map.73 = (bf16[128,2,16,128]{3,2,1,0:T(8,128)(2,1)S(1)}, f32[2048,128]{1,0:T(8,128)S(1)}, f32[2,2,128]{2,1,0:T(2,128)S(1)}) custom-call(bf16[2048,128]{1,0:T(8,128)(2,1)} %bitcast.17, bf16[8,128,128]{2,1,0:T(8,128)(2,1)} %bitcast.21, bf16[2,128,128]{2,1,0:T(8,128)(2,1)} %rest_1_.1, f32[2,128]{1,0:T(2,128)} %gain_hbm.1, f32[2,128]{1,0:T(2,128)} %out_gain_hbm.1), custom_call_target="tpu_custom_call" | custom-call | tf_op jit(solution)/shard_map/pallas_call | solution.py:265
  2.5 0.0 copy-start.1
  2.6 30.2 %all_to_all.20 = bf16[128,32,128]{2,1,0:T(8,128)(2,1)S(1)} all-to-all(bf16[128,32,128]{2,1,0:T(8,128)(2,1)S(1)} %bitcast.20), channel_id=1, replica_groups=mesh['y_hi'=2,'y_lo'=2,'z_lo'=2,'x_hi'=2,'x_lo'=2,'z_hi'=2,'core'=2] {'y..., dimensions={0} | all-to-all | bytes 2097152 | tf_op jit(solution)/shard_map/all_to_all | solution.py:285
  32.8 0.0 copy-done.1
  32.8 1.1 %shard_map.74 = bf16[2048,128]{1,0:T(8,128)(2,1)S(1)} custom-call(bf16[4096,128]{1,0:T(8,128)(2,1)S(1)} %bitcast.12, bf16[512,512]{1,0:T(8,128)(2,1)S(1)} %copy-done.1), custom_call_target="tpu_custom_call" | custom-call | tf_op jit(solution)/shard_map/pallas_call | solution.py:265
  33.9 0.0 copy-start
  33.9 0.0 copy-start.2
  33.9 0.0 copy-start.3
  33.9 0.0 copy-start.4
  33.9 17.8 %all_to_all.21 = bf16[128,16,128]{2,1,0:T(8,128)(2,1)S(1)} all-to-all(bf16[128,16,128]{2,1,0:T(8,128)(2,1)S(1)} %bitcast.16), channel_id=1, replica_groups=mesh['y_hi'=2,'y_lo'=2,'z_lo'=2,'x_hi'=2,'x_lo'=2,'z_hi'=2,'core'=2] {'y..., dimensions={0} | all-to-all | bytes 1048576 | tf_op jit(solution)/shard_map/all_to_all | solution.py:285
  51.7 0.0 copy-done
  51.7 0.0 copy-done.2
  51.7 0.0 copy-done.3
  51.7 0.0 copy-done.4
  51.7 1.8 %shard_map.75 = (bf16[2048,128]{1,0:T(8,128)(2,1)S(1)}, bf16[128,2,16,128]{3,2,1,0:T(8,128)(2,1)S(1)}, f32[2048,128]{1,0:T(8,128)S(1)}) custom-call(bf16[2048,128]{1,0:T(8,128)(2,1)S(1)} %bitcast.13, bf16[2048,128]{1,0:T(8,128)(2,1)S(1)} %bitcast.18, f32[2048,128]{1,0:T(8,128)S(1)} %get-tuple-element.12.gate_ref, bf16[2,128,128]{2,1,0:T(8,128)(2,1)S(1)} %copy-done.3, ...), custom_call_target="tpu_custom_call" | custom-call | tf_op jit(solution)/shard_map/pallas_call | solution.py:265
  53.5 23.0 %all_to_all.22 = bf16[128,32,128]{2,1,0:T(8,128)(2,1)S(1)} all-to-all(bf16[128,32,128]{2,1,0:T(8,128)(2,1)S(1)} %bitcast.19), channel_id=1, replica_groups=mesh['y_hi'=2,'y_lo'=2,'z_lo'=2,'x_hi'=2,'x_lo'=2,'z_hi'=2,'core'=2] {'y..., dimensions={0} | all-to-all | bytes 2097152 | tf_op jit(solution)/shard_map/all_to_all | solution.py:285
  76.5 1.0 %shard_map.76 = bf16[2048,128]{1,0:T(8,128)(2,1)S(1)} custom-call(bf16[4096,128]{1,0:T(8,128)(2,1)S(1)} %bitcast.11, bf16[512,512]{1,0:T(8,128)(2,1)S(1)} %copy-done.1), custom_call_target="tpu_custom_call" | custom-call | tf_op jit(solution)/shard_map/pallas_call | solution.py:265
  77.6 17.6 %all_to_all.23 = bf16[128,16,128]{2,1,0:T(8,128)(2,1)S(1)} all-to-all(bf16[128,16,128]{2,1,0:T(8,128)(2,1)S(1)} %bitcast.15), channel_id=1, replica_groups=mesh['y_hi'=2,'y_lo'=2,'z_lo'=2,'x_hi'=2,'x_lo'=2,'z_hi'=2,'core'=2] {'y..., dimensions={0} | all-to-all | bytes 1048576 | tf_op jit(solution)/shard_map/all_to_all | solution.py:285
  95.2 1.4 %shard_map.77 = bf16[4,16,32,128]{3,2,1,0:T(8,128)(2,1)} custom-call(bf16[2048,128]{1,0:T(8,128)(2,1)S(1)} %bitcast.14, bf16[2048,128]{1,0:T(8,128)(2,1)S(1)} %get-tuple-element.15.pair_ref, f32[2048,128]{1,0:T(8,128)S(1)} %get-tuple-element.16.gate_ref, bf16[2,128,128]{2,1,0:T(8,128)(2,1)S(1)} %copy-done.3, f32[2,2,128]{2,1,0:T(2,128)S(1)} %get-tuple-element.13.gain_ref), custom_call_target="tpu_custom_call" | custom-call | tf_op jit(solution)/shard_map/pallas_call | solution.py:265
Async XLA Ops:
  2.5 30.2 %copy-start.1 = (bf16[512,512]{1,0:T(8,128)(2,1)S(1)}, bf16[512,512]{1,0:T(8,128)(2,1)}, u32[]{:S(2)}) copy-start(bf16[512,512]{1,0:T(8,128)(2,1)} %constant.2.clone.regroup_ref) | copy-start | bytes 1572868
  33.9 17.8 %copy-start = (bf16[64,32,128]{2,1,0:T(8,128)(2,1)S(1)}, bf16[64,32,128]{2,1,0:T(8,128)(2,1)}, u32[]{:S(2)}) copy-start(bf16[64,32,128]{2,1,0:T(8,128)(2,1)} %param.7) | copy-start | bytes 1572868
  33.9 17.8 %copy-start.2 = (bf16[2,2,2,128,128]{4,3,2,1,0:T(8,128)(2,1)S(1)}, bf16[2,2,2,128,128]{4,3,2,1,0:T(8,128)(2,1)}, u32[]{:S(2)}) copy-start(bf16[2,2,2,128,128]{4,3,2,1,0:T(8,128)(2,1)} %param.8) | copy-start | bytes 786436
  33.9 17.8 %copy-start.3 = (bf16[2,128,128]{2,1,0:T(8,128)(2,1)S(1)}, bf16[2,128,128]{2,1,0:T(8,128)(2,1)}, u32[]{:S(2)}) copy-start(bf16[2,128,128]{2,1,0:T(8,128)(2,1)} %out_weight_ref.3) | copy-start | bytes 196612
  33.9 17.8 %copy-start.4 = (bf16[2,128,128]{2,1,0:T(8,128)(2,1)S(1)}, bf16[2,128,128]{2,1,0:T(8,128)(2,1)}, u32[]{:S(2)}) copy-start(bf16[2,128,128]{2,1,0:T(8,128)(2,1)} %rest_1_.1) | copy-start | bytes 196612

commit v4 on v3

--- a/solution.py
+++ b/solution.py
@@ -45,16 +45,20 @@
     return jnp.concatenate([ref[n : n + 512, :], ref[n + 512 : n + 1024, :]], axis=1)
 
 
-def norm_rows(pair_ref, arrive, gain, centred_ref, normed_ref):
+def norm_rows(pair_ref, gain, centred_ref, normed_ref, lanes):
     row = lax.broadcasted_iota(jnp.int32, (128, 128), 0)
     column = lax.broadcasted_iota(jnp.int32, (128, 128), 1)
     centring = two_blocks(jnp.where(row == column, 127.0 / 128.0, -1.0 / 128.0).astype(BF16))
     average = two_blocks(jnp.full((128, 128), 1.0 / 128.0, BF16))
     for n in range(0, 2048, 1024):
-        arrive(n)
-        centred_ref[n // 2 : n // 2 + 512, :] = dot(side_by_side(pair_ref, n), centring, ((1,), (0,)))
-
-    gains = jnp.concatenate([gain(), gain()], axis=1)
+        if lanes:
+            for m in range(2):
+                values = pair_ref[n + 512 * m : n + 512 * m + 512, :].astype(F32)
+                centred = values - jnp.mean(values, axis=1, keepdims=True)
+                centred_ref[n // 2 : n // 2 + 512, 128 * m : 128 * m + 128] = centred
+        else:
+            centred_ref[n // 2 : n // 2 + 512, :] = dot(side_by_side(pair_ref, n), centring, ((1,), (0,)))
+    gains = jnp.concatenate([gain, gain], axis=1)
 
     def spread(n):
         centred = centred_ref[n // 2 : n // 2 + 512, :]
@@ -68,9 +72,9 @@
     ahead(range(0, 2048, 1024), spread, scale)
 
 
-def project(pair_ref, arrive, gain, wt_ref, gate_weight, refs, out_ref, gate_ref):
+def project(pair_ref, gain, wt_ref, gate_weight, refs, out_ref, gate_ref, lanes=False):
     centred_ref, normed_ref, half_ref = refs
-    norm_rows(pair_ref, arrive, gain, centred_ref, normed_ref)
+    norm_rows(pair_ref, gain, centred_ref, normed_ref, lanes)
     slabs = normed_ref.reshape(4, 16, 32, 128)
     def product(place):
         s, side = place
@@ -84,7 +88,7 @@
             half_ref[pl.ds(side * 16 + s + n, 128, stride=40), :] = result[:, 128 * n : 128 * n + 128]
 
     ahead([(s, side) for s in range(0, 16, 2) for side in range(2)], product, gated)
-    weight = two_blocks(halved(gate_weight()))
+    weight = two_blocks(halved(gate_weight))
 
     def gate_product(n):
         return dot(side_by_side(normed_ref, n), weight, ((1,), (0,)))
@@ -117,28 +121,22 @@
     pair_hbm, side_hbm, gate_weight_hbm, gain_hbm, out_gain_hbm, out_ref, gate_ref, gain_ref, pair_ref, side_ref, gate_weight_ref,
     wt_ref, centred_ref, normed_ref, half_ref, sems,
 ):
-    halves = [pl.ds(n, 1024) for n in (0, 1024)]
     copies = [
-        *[pltpu.make_async_copy(pair_hbm.at[half], pair_ref.at[half], sems.at[n]) for n, half in enumerate(halves)],
-        pltpu.make_async_copy(side_hbm.at[pl.ds(0, 4)], side_ref, sems.at[2]),
-        pltpu.make_async_copy(gate_weight_hbm.at[0], gate_weight_ref, sems.at[3]),
-        pltpu.make_async_copy(gain_hbm, gain_ref.at[0], sems.at[4]),
-        pltpu.make_async_copy(out_gain_hbm, gain_ref.at[1], sems.at[5]),
+        pltpu.make_async_copy(side_hbm.at[pl.ds(0, 4)], side_ref, sems.at[0]),
+        pltpu.make_async_copy(pair_hbm, pair_ref, sems.at[1]),
+        pltpu.make_async_copy(gate_weight_hbm.at[0], gate_weight_ref, sems.at[2]),
+        pltpu.make_async_copy(gain_hbm, gain_ref.at[0], sems.at[3]),
+        pltpu.make_async_copy(out_gain_hbm, gain_ref.at[1], sems.at[4]),
     ]
     for copy in copies:
         copy.start()
-
-    def arrive(n):
-        if n == 0:
-            copies[0].wait()
-        else:
-            for copy in copies[1:]:
-                copy.wait()
-            fill_weights(side_ref, wt_ref, 0)
-
+    copies[0].wait()
+    fill_weights(side_ref, wt_ref, 0)
+    for copy in copies[1:]:
+        copy.wait()
     project(
-        pair_ref, arrive, lambda: gain_ref[0, 0:1, :], wt_ref, lambda: gate_weight_ref[...],
-        (centred_ref, normed_ref, half_ref), out_ref, gate_ref,
+        pair_ref, gain_ref[0, 0:1, :], wt_ref, gate_weight_ref[...],
+        (centred_ref, normed_ref, half_ref), out_ref, gate_ref, True,
     )
 
 
@@ -254,7 +252,7 @@
         copy.wait()
     if update == 0:
         project(
-            pair_out_ref, lambda n: None, lambda: gain_ref[0, 1:2, :], wt_ref, lambda: gate_weight_ref[1],
+            pair_out_ref, gain_ref[0, 1:2, :], wt_ref, gate_weight_ref[1],
             (centred_ref, normed_ref, half_ref), out_ref, gate_out_ref,
         )
 
@@ -292,7 +290,7 @@
     sides, gate, gains = call(
         project_kernel,
         [SIDES, GATE, GAIN],
-        [PAIR, ((4, 128, 128), BF16), ((128, 128), BF16), *PROJECT_SCRATCH, pltpu.SemaphoreType.DMA((6,))],
+        [PAIR, ((4, 128, 128), BF16), ((128, 128), BF16), *PROJECT_SCRATCH, pltpu.SemaphoreType.DMA((5,))],
         pair, side_weight, gate_weight, in_gain, out_gain,
         hbm=range(5),
     )

time: 96.8 us -> 96.7 us (level)
  no operation moved by 1% of the time
where the time goes in v4:
time: 96.7 us; the launch traced here: 96.4 us
  blocking collectives  88.6 us (92%)
  Pallas kernels  7.71 us (8%)
    all_to_all x4, blocking collectives, exchange(): lax.all_to_all(pieces, ORDER, split_axis=0, concat_axis=0, tiled=True)  88.6 us
    pallas_call x5, Pallas kernels, call(): pl.pallas_call(kernel, out_shape=[jax.ShapeDtypeStruct(*one) for one in o...  7.71 us

profile of v4, /device:TPU:1, one launch (start us, length us, event | category | flops | bytes accessed | tf_op | source)
XLA Modules:
  0.0 96.4 jit_solution(3456830955491600642)
XLA Ops:
  0.0 2.4 %shard_map.73 = (bf16[128,2,16,128]{3,2,1,0:T(8,128)(2,1)S(1)}, f32[2048,128]{1,0:T(8,128)S(1)}, f32[2,2,128]{2,1,0:T(2,128)S(1)}) custom-call(bf16[2048,128]{1,0:T(8,128)(2,1)} %bitcast.17, bf16[8,128,128]{2,1,0:T(8,128)(2,1)} %bitcast.21, bf16[2,128,128]{2,1,0:T(8,128)(2,1)} %rest_1_.1, f32[2,128]{1,0:T(2,128)} %gain_hbm.1, f32[2,128]{1,0:T(2,128)} %out_gain_hbm.1), custom_call_target="tpu_custom_call" | custom-call | tf_op jit(solution)/shard_map/pallas_call | solution.py:263
  2.4 0.0 copy-start.1
  2.4 30.2 %all_to_all.20 = bf16[128,32,128]{2,1,0:T(8,128)(2,1)S(1)} all-to-all(bf16[128,32,128]{2,1,0:T(8,128)(2,1)S(1)} %bitcast.20), channel_id=1, replica_groups=mesh['y_hi'=2,'y_lo'=2,'z_lo'=2,'x_hi'=2,'x_lo'=2,'z_hi'=2,'core'=2] {'y..., dimensions={0} | all-to-all | bytes 2097152 | tf_op jit(solution)/shard_map/all_to_all | solution.py:283
  32.7 0.0 copy-done.1
  32.7 1.1 %shard_map.74 = bf16[2048,128]{1,0:T(8,128)(2,1)S(1)} custom-call(bf16[4096,128]{1,0:T(8,128)(2,1)S(1)} %bitcast.12, bf16[512,512]{1,0:T(8,128)(2,1)S(1)} %copy-done.1), custom_call_target="tpu_custom_call" | custom-call | tf_op jit(solution)/shard_map/pallas_call | solution.py:263
  33.7 0.0 copy-start
  33.8 0.0 copy-start.2
  33.8 0.0 copy-start.3
  33.8 0.0 copy-start.4
  33.8 17.8 %all_to_all.21 = bf16[128,16,128]{2,1,0:T(8,128)(2,1)S(1)} all-to-all(bf16[128,16,128]{2,1,0:T(8,128)(2,1)S(1)} %bitcast.16), channel_id=1, replica_groups=mesh['y_hi'=2,'y_lo'=2,'z_lo'=2,'x_hi'=2,'x_lo'=2,'z_hi'=2,'core'=2] {'y..., dimensions={0} | all-to-all | bytes 1048576 | tf_op jit(solution)/shard_map/all_to_all | solution.py:283
  51.6 0.0 copy-done
  51.6 0.0 copy-done.2
  51.6 0.0 copy-done.3
  51.6 0.0 copy-done.4
  51.6 1.8 %shard_map.75 = (bf16[2048,128]{1,0:T(8,128)(2,1)S(1)}, bf16[128,2,16,128]{3,2,1,0:T(8,128)(2,1)S(1)}, f32[2048,128]{1,0:T(8,128)S(1)}) custom-call(bf16[2048,128]{1,0:T(8,128)(2,1)S(1)} %bitcast.13, bf16[2048,128]{1,0:T(8,128)(2,1)S(1)} %bitcast.18, f32[2048,128]{1,0:T(8,128)S(1)} %get-tuple-element.12.gate_ref, bf16[2,128,128]{2,1,0:T(8,128)(2,1)S(1)} %copy-done.3, ...), custom_call_target="tpu_custom_call" | custom-call | tf_op jit(solution)/shard_map/pallas_call | solution.py:263
  53.4 23.0 %all_to_all.22 = bf16[128,32,128]{2,1,0:T(8,128)(2,1)S(1)} all-to-all(bf16[128,32,128]{2,1,0:T(8,128)(2,1)S(1)} %bitcast.19), channel_id=1, replica_groups=mesh['y_hi'=2,'y_lo'=2,'z_lo'=2,'x_hi'=2,'x_lo'=2,'z_hi'=2,'core'=2] {'y..., dimensions={0} | all-to-all | bytes 2097152 | tf_op jit(solution)/shard_map/all_to_all | solution.py:283
  76.4 1.0 %shard_map.76 = bf16[2048,128]{1,0:T(8,128)(2,1)S(1)} custom-call(bf16[4096,128]{1,0:T(8,128)(2,1)S(1)} %bitcast.11, bf16[512,512]{1,0:T(8,128)(2,1)S(1)} %copy-done.1), custom_call_target="tpu_custom_call" | custom-call | tf_op jit(solution)/shard_map/pallas_call | solution.py:263
  77.4 17.6 %all_to_all.23 = bf16[128,16,128]{2,1,0:T(8,128)(2,1)S(1)} all-to-all(bf16[128,16,128]{2,1,0:T(8,128)(2,1)S(1)} %bitcast.15), channel_id=1, replica_groups=mesh['y_hi'=2,'y_lo'=2,'z_lo'=2,'x_hi'=2,'x_lo'=2,'z_hi'=2,'core'=2] {'y..., dimensions={0} | all-to-all | bytes 1048576 | tf_op jit(solution)/shard_map/all_to_all | solution.py:283
  95.1 1.4 %shard_map.77 = bf16[4,16,32,128]{3,2,1,0:T(8,128)(2,1)} custom-call(bf16[2048,128]{1,0:T(8,128)(2,1)S(1)} %bitcast.14, bf16[2048,128]{1,0:T(8,128)(2,1)S(1)} %get-tuple-element.15.pair_ref, f32[2048,128]{1,0:T(8,128)S(1)} %get-tuple-element.16.gate_ref, bf16[2,128,128]{2,1,0:T(8,128)(2,1)S(1)} %copy-done.3, f32[2,2,128]{2,1,0:T(2,128)S(1)} %get-tuple-element.13.gain_ref), custom_call_target="tpu_custom_call" | custom-call | tf_op jit(solution)/shard_map/pallas_call | solution.py:263
Async XLA Ops:
  2.4 30.2 %copy-start.1 = (bf16[512,512]{1,0:T(8,128)(2,1)S(1)}, bf16[512,512]{1,0:T(8,128)(2,1)}, u32[]{:S(2)}) copy-start(bf16[512,512]{1,0:T(8,128)(2,1)} %constant.2.clone.regroup_ref) | copy-start | bytes 1572868
  33.7 17.8 %copy-start = (bf16[64,32,128]{2,1,0:T(8,128)(2,1)S(1)}, bf16[64,32,128]{2,1,0:T(8,128)(2,1)}, u32[]{:S(2)}) copy-start(bf16[64,32,128]{2,1,0:T(8,128)(2,1)} %param.7) | copy-start | bytes 1572868
  33.8 17.8 %copy-start.2 = (bf16[2,2,2,128,128]{4,3,2,1,0:T(8,128)(2,1)S(1)}, bf16[2,2,2,128,128]{4,3,2,1,0:T(8,128)(2,1)}, u32[]{:S(2)}) copy-start(bf16[2,2,2,128,128]{4,3,2,1,0:T(8,128)(2,1)} %param.8) | copy-start | bytes 786436
  33.8 17.8 %copy-start.3 = (bf16[2,128,128]{2,1,0:T(8,128)(2,1)S(1)}, bf16[2,128,128]{2,1,0:T(8,128)(2,1)}, u32[]{:S(2)}) copy-start(bf16[2,128,128]{2,1,0:T(8,128)(2,1)} %out_weight_ref.3) | copy-start | bytes 196612
  33.8 17.8 %copy-start.4 = (bf16[2,128,128]{2,1,0:T(8,128)(2,1)S(1)}, bf16[2,128,128]{2,1,0:T(8,128)(2,1)}, u32[]{:S(2)}) copy-start(bf16[2,128,128]{2,1,0:T(8,128)(2,1)} %rest_1_.1) | copy-start | bytes 196612

commit v5 on v4

--- a/solution.py
+++ b/solution.py
@@ -46,25 +46,27 @@
 
 
 def norm_rows(pair_ref, gain, centred_ref, normed_ref, lanes):
-    row = lax.broadcasted_iota(jnp.int32, (128, 128), 0)
-    column = lax.broadcasted_iota(jnp.int32, (128, 128), 1)
-    centring = two_blocks(jnp.where(row == column, 127.0 / 128.0, -1.0 / 128.0).astype(BF16))
     average = two_blocks(jnp.full((128, 128), 1.0 / 128.0, BF16))
-    for n in range(0, 2048, 1024):
+    for n in range(0, 2048, 512):
+        values = pair_ref[n : n + 512, :].astype(F32)
+        row, lane = n // 1024 * 512, n % 1024 // 512 * 128
+        centred_ref[row : row + 512, lane : lane + 128] = values - jnp.mean(values, axis=1, keepdims=True)
+    gains = jnp.concatenate([gain, gain], axis=1)
+
+    def spread(n):
+        centred = centred_ref[n // 2 : n // 2 + 512, :]
+        square = centred * centred
+        if lanes:
+            return [jnp.mean(square[:, m : m + 128], axis=1, keepdims=True) for m in (0, 128)]
+        return dot(square.astype(BF16), average, ((1,), (0,)))
+
+    def scale(n, variance):
         if lanes:
             for m in range(2):
-                values = pair_ref[n + 512 * m : n + 512 * m + 512, :].astype(F32)
-                centred = values - jnp.mean(values, axis=1, keepdims=True)
-                centred_ref[n // 2 : n // 2 + 512, 128 * m : 128 * m + 128] = centred
-        else:
-            centred_ref[n // 2 : n // 2 + 512, :] = dot(side_by_side(pair_ref, n), centring, ((1,), (0,)))
-    gains = jnp.concatenate([gain, gain], axis=1)
-
-    def spread(n):
-        centred = centred_ref[n // 2 : n // 2 + 512, :]
-        return dot((centred * centred).astype(BF16), average, ((1,), (0,)))
-
-    def scale(n, variance):
+                centred = centred_ref[n // 2 : n // 2 + 512, 128 * m : 128 * m + 128]
+                normed = (centred * lax.rsqrt(variance[m] + epsilon) * gain).astype(BF16)
+                normed_ref[n + 512 * m : n + 512 * m + 512, :] = normed
+            return
         normed = (centred_ref[n // 2 : n // 2 + 512, :] * lax.rsqrt(variance + epsilon) * gains).astype(BF16)
         normed_ref[n : n + 512, :] = normed[:, :128]
         normed_ref[n + 512 : n + 1024, :] = normed[:, 128:]
@@ -72,7 +74,7 @@
     ahead(range(0, 2048, 1024), spread, scale)
 
 
-def project(pair_ref, gain, wt_ref, gate_weight, refs, out_ref, gate_ref, lanes=False):
+def project(pair_ref, gain, wt_ref, gate_weight, refs, out_ref, gate_ref, lanes):
     centred_ref, normed_ref, half_ref = refs
     norm_rows(pair_ref, gain, centred_ref, normed_ref, lanes)
     slabs = normed_ref.reshape(4, 16, 32, 128)
@@ -136,7 +138,7 @@
         copy.wait()
     project(
         pair_ref, gain_ref[0, 0:1, :], wt_ref, gate_weight_ref[...],
-        (centred_ref, normed_ref, half_ref), out_ref, gate_ref, True,
+        (centred_ref, normed_ref, half_ref), out_ref, gate_ref, False,
     )
 
 
@@ -253,7 +255,7 @@
     if update == 0:
         project(
             pair_out_ref, gain_ref[0, 1:2, :], wt_ref, gate_weight_ref[1],
-            (centred_ref, normed_ref, half_ref), out_ref, gate_out_ref,
+            (centred_ref, normed_ref, half_ref), out_ref, gate_out_ref, True,
         )
 
 

time: 96.7 us -> 97.1 us (level)
  no operation moved by 1% of the time
where the time goes in v5:
time: 97.1 us; the launch traced here: 96.9 us
  blocking collectives  88.6 us (91%)
  Pallas kernels  8.2 us (8%)
    all_to_all x4, blocking collectives, exchange(): lax.all_to_all(pieces, ORDER, split_axis=0, concat_axis=0, tiled=True)  88.6 us
    pallas_call x5, Pallas kernels, call(): pl.pallas_call(kernel, out_shape=[jax.ShapeDtypeStruct(*one) for one in o...  8.2 us

profile of v5, /device:TPU:1, one launch (start us, length us, event | category | flops | bytes accessed | tf_op | source)
XLA Modules:
  0.0 96.9 jit_solution(7869288498464021786)
XLA Ops:
  0.0 2.4 %shard_map.73 = (bf16[128,2,16,128]{3,2,1,0:T(8,128)(2,1)S(1)}, f32[2048,128]{1,0:T(8,128)S(1)}, f32[2,2,128]{2,1,0:T(2,128)S(1)}) custom-call(bf16[2048,128]{1,0:T(8,128)(2,1)} %bitcast.17, bf16[8,128,128]{2,1,0:T(8,128)(2,1)} %bitcast.21, bf16[2,128,128]{2,1,0:T(8,128)(2,1)} %rest_1_.1, f32[2,128]{1,0:T(2,128)} %gain_hbm.1, f32[2,128]{1,0:T(2,128)} %out_gain_hbm.1), custom_call_target="tpu_custom_call" | custom-call | tf_op jit(solution)/shard_map/pallas_call | solution.py:265
  2.4 0.0 copy-start.1
  2.4 30.2 %all_to_all.20 = bf16[128,32,128]{2,1,0:T(8,128)(2,1)S(1)} all-to-all(bf16[128,32,128]{2,1,0:T(8,128)(2,1)S(1)} %bitcast.20), channel_id=1, replica_groups=mesh['y_hi'=2,'y_lo'=2,'z_lo'=2,'x_hi'=2,'x_lo'=2,'z_hi'=2,'core'=2] {'y..., dimensions={0} | all-to-all | bytes 2097152 | tf_op jit(solution)/shard_map/all_to_all | solution.py:285
  32.7 0.0 copy-done.1
  32.7 1.1 %shard_map.74 = bf16[2048,128]{1,0:T(8,128)(2,1)S(1)} custom-call(bf16[4096,128]{1,0:T(8,128)(2,1)S(1)} %bitcast.12, bf16[512,512]{1,0:T(8,128)(2,1)S(1)} %copy-done.1), custom_call_target="tpu_custom_call" | custom-call | tf_op jit(solution)/shard_map/pallas_call | solution.py:265
  33.7 0.0 copy-start
  33.8 0.0 copy-start.2
  33.8 0.0 copy-start.3
  33.8 0.0 copy-start.4
  33.8 17.8 %all_to_all.21 = bf16[128,16,128]{2,1,0:T(8,128)(2,1)S(1)} all-to-all(bf16[128,16,128]{2,1,0:T(8,128)(2,1)S(1)} %bitcast.16), channel_id=1, replica_groups=mesh['y_hi'=2,'y_lo'=2,'z_lo'=2,'x_hi'=2,'x_lo'=2,'z_hi'=2,'core'=2] {'y..., dimensions={0} | all-to-all | bytes 1048576 | tf_op jit(solution)/shard_map/all_to_all | solution.py:285
  51.6 0.0 copy-done
  51.6 0.0 copy-done.2
  51.6 0.0 copy-done.3
  51.6 0.0 copy-done.4
  51.6 2.3 %shard_map.75 = (bf16[2048,128]{1,0:T(8,128)(2,1)S(1)}, bf16[128,2,16,128]{3,2,1,0:T(8,128)(2,1)S(1)}, f32[2048,128]{1,0:T(8,128)S(1)}) custom-call(bf16[2048,128]{1,0:T(8,128)(2,1)S(1)} %bitcast.13, bf16[2048,128]{1,0:T(8,128)(2,1)S(1)} %bitcast.18, f32[2048,128]{1,0:T(8,128)S(1)} %get-tuple-element.12.gate_ref, bf16[2,128,128]{2,1,0:T(8,128)(2,1)S(1)} %copy-done.3, ...), custom_call_target="tpu_custom_call" | custom-call | tf_op jit(solution)/shard_map/pallas_call | solution.py:265
  53.9 23.0 %all_to_all.22 = bf16[128,32,128]{2,1,0:T(8,128)(2,1)S(1)} all-to-all(bf16[128,32,128]{2,1,0:T(8,128)(2,1)S(1)} %bitcast.19), channel_id=1, replica_groups=mesh['y_hi'=2,'y_lo'=2,'z_lo'=2,'x_hi'=2,'x_lo'=2,'z_hi'=2,'core'=2] {'y..., dimensions={0} | all-to-all | bytes 2097152 | tf_op jit(solution)/shard_map/all_to_all | solution.py:285
  76.9 1.0 %shard_map.76 = bf16[2048,128]{1,0:T(8,128)(2,1)S(1)} custom-call(bf16[4096,128]{1,0:T(8,128)(2,1)S(1)} %bitcast.11, bf16[512,512]{1,0:T(8,128)(2,1)S(1)} %copy-done.1), custom_call_target="tpu_custom_call" | custom-call | tf_op jit(solution)/shard_map/pallas_call | solution.py:265
  77.9 17.6 %all_to_all.23 = bf16[128,16,128]{2,1,0:T(8,128)(2,1)S(1)} all-to-all(bf16[128,16,128]{2,1,0:T(8,128)(2,1)S(1)} %bitcast.15), channel_id=1, replica_groups=mesh['y_hi'=2,'y_lo'=2,'z_lo'=2,'x_hi'=2,'x_lo'=2,'z_hi'=2,'core'=2] {'y..., dimensions={0} | all-to-all | bytes 1048576 | tf_op jit(solution)/shard_map/all_to_all | solution.py:285
  95.6 1.4 %shard_map.77 = bf16[4,16,32,128]{3,2,1,0:T(8,128)(2,1)} custom-call(bf16[2048,128]{1,0:T(8,128)(2,1)S(1)} %bitcast.14, bf16[2048,128]{1,0:T(8,128)(2,1)S(1)} %get-tuple-element.15.pair_ref, f32[2048,128]{1,0:T(8,128)S(1)} %get-tuple-element.16.gate_ref, bf16[2,128,128]{2,1,0:T(8,128)(2,1)S(1)} %copy-done.3, f32[2,2,128]{2,1,0:T(2,128)S(1)} %get-tuple-element.13.gain_ref), custom_call_target="tpu_custom_call" | custom-call | tf_op jit(solution)/shard_map/pallas_call | solution.py:265
Async XLA Ops:
  2.4 30.2 %copy-start.1 = (bf16[512,512]{1,0:T(8,128)(2,1)S(1)}, bf16[512,512]{1,0:T(8,128)(2,1)}, u32[]{:S(2)}) copy-start(bf16[512,512]{1,0:T(8,128)(2,1)} %constant.2.clone.regroup_ref) | copy-start | bytes 1572868
  33.7 17.8 %copy-start = (bf16[64,32,128]{2,1,0:T(8,128)(2,1)S(1)}, bf16[64,32,128]{2,1,0:T(8,128)(2,1)}, u32[]{:S(2)}) copy-start(bf16[64,32,128]{2,1,0:T(8,128)(2,1)} %param.7) | copy-start | bytes 1572868
  33.8 17.8 %copy-start.2 = (bf16[2,2,2,128,128]{4,3,2,1,0:T(8,128)(2,1)S(1)}, bf16[2,2,2,128,128]{4,3,2,1,0:T(8,128)(2,1)}, u32[]{:S(2)}) copy-start(bf16[2,2,2,128,128]{4,3,2,1,0:T(8,128)(2,1)} %param.8) | copy-start | bytes 786436
  33.8 17.8 %copy-start.3 = (bf16[2,128,128]{2,1,0:T(8,128)(2,1)S(1)}, bf16[2,128,128]{2,1,0:T(8,128)(2,1)}, u32[]{:S(2)}) copy-start(bf16[2,128,128]{2,1,0:T(8,128)(2,1)} %out_weight_ref.3) | copy-start | bytes 196612
  33.8 17.8 %copy-start.4 = (bf16[2,128,128]{2,1,0:T(8,128)(2,1)S(1)}, bf16[2,128,128]{2,1,0:T(8,128)(2,1)}, u32[]{:S(2)}) copy-start(bf16[2,128,128]{2,1,0:T(8,128)(2,1)} %rest_1_.1) | copy-start | bytes 196612

commit v6 on v4

--- a/solution.py
+++ b/solution.py
@@ -45,19 +45,14 @@
     return jnp.concatenate([ref[n : n + 512, :], ref[n + 512 : n + 1024, :]], axis=1)
 
 
-def norm_rows(pair_ref, gain, centred_ref, normed_ref, lanes):
+def norm_rows(pair_ref, gain, centred_ref, normed_ref, prepare):
     row = lax.broadcasted_iota(jnp.int32, (128, 128), 0)
     column = lax.broadcasted_iota(jnp.int32, (128, 128), 1)
     centring = two_blocks(jnp.where(row == column, 127.0 / 128.0, -1.0 / 128.0).astype(BF16))
     average = two_blocks(jnp.full((128, 128), 1.0 / 128.0, BF16))
     for n in range(0, 2048, 1024):
-        if lanes:
-            for m in range(2):
-                values = pair_ref[n + 512 * m : n + 512 * m + 512, :].astype(F32)
-                centred = values - jnp.mean(values, axis=1, keepdims=True)
-                centred_ref[n // 2 : n // 2 + 512, 128 * m : 128 * m + 128] = centred
-        else:
-            centred_ref[n // 2 : n // 2 + 512, :] = dot(side_by_side(pair_ref, n), centring, ((1,), (0,)))
+        centred_ref[n // 2 : n // 2 + 512, :] = dot(side_by_side(pair_ref, n), centring, ((1,), (0,)))
+    prepare()
     gains = jnp.concatenate([gain, gain], axis=1)
 
     def spread(n):
@@ -72,9 +67,9 @@
     ahead(range(0, 2048, 1024), spread, scale)
 
 
-def project(pair_ref, gain, wt_ref, gate_weight, refs, out_ref, gate_ref, lanes=False):
+def project(pair_ref, gain, wt_ref, gate_weight, refs, out_ref, gate_ref, prepare):
     centred_ref, normed_ref, half_ref = refs
-    norm_rows(pair_ref, gain, centred_ref, normed_ref, lanes)
+    norm_rows(pair_ref, gain, centred_ref, normed_ref, prepare)
     slabs = normed_ref.reshape(4, 16, 32, 128)
     def product(place):
         s, side = place
@@ -136,7 +131,7 @@
         copy.wait()
     project(
         pair_ref, gain_ref[0, 0:1, :], wt_ref, gate_weight_ref[...],
-        (centred_ref, normed_ref, half_ref), out_ref, gate_ref, True,
+        (centred_ref, normed_ref, half_ref), out_ref, gate_ref, lambda: None,
     )
 
 
@@ -220,8 +215,6 @@
          normed_ref, half_ref) = rest
     else:
         pair_hbm, raw_ref, pair_out_ref, sems = rest
-    if update == 0:
-        fill_weights(side_ref, wt_ref, 1)
     for channel in range(0, 128, 16):
         part = mixed_ref[16 * channel : 16 * channel + 256, :].astype(F32).reshape(16, 16, 128)
         for n in range(16):
@@ -254,6 +247,7 @@
         project(
             pair_out_ref, gain_ref[0, 1:2, :], wt_ref, gate_weight_ref[1],
             (centred_ref, normed_ref, half_ref), out_ref, gate_out_ref,
+            lambda: fill_weights(side_ref, wt_ref, 1),
         )
 
 

time: 96.7 us -> 96.7 us (level)
  no operation moved by 1% of the time
where the time goes in v6:
time: 96.7 us; the launch traced here: 96.5 us
  blocking collectives  88.6 us (92%)
  Pallas kernels  7.73 us (8%)
    all_to_all x4, blocking collectives, exchange(): lax.all_to_all(pieces, ORDER, split_axis=0, concat_axis=0, tiled=True)  88.6 us
    pallas_call x5, Pallas kernels, call(): pl.pallas_call(kernel, out_shape=[jax.ShapeDtypeStruct(*one) for one in o...  7.73 us

profile of v6, /device:TPU:1, one launch (start us, length us, event | category | flops | bytes accessed | tf_op | source)
XLA Modules:
  0.0 96.5 jit_solution(14482149773353896939)
XLA Ops:
  0.0 2.4 %shard_map.73 = (bf16[128,2,16,128]{3,2,1,0:T(8,128)(2,1)S(1)}, f32[2048,128]{1,0:T(8,128)S(1)}, f32[2,2,128]{2,1,0:T(2,128)S(1)}) custom-call(bf16[2048,128]{1,0:T(8,128)(2,1)} %bitcast.17, bf16[8,128,128]{2,1,0:T(8,128)(2,1)} %bitcast.21, bf16[2,128,128]{2,1,0:T(8,128)(2,1)} %rest_1_.1, f32[2,128]{1,0:T(2,128)} %gain_hbm.1, f32[2,128]{1,0:T(2,128)} %out_gain_hbm.1), custom_call_target="tpu_custom_call" | custom-call | tf_op jit(solution)/shard_map/pallas_call | solution.py:257
  2.4 0.0 copy-start.1
  2.5 30.2 %all_to_all.20 = bf16[128,32,128]{2,1,0:T(8,128)(2,1)S(1)} all-to-all(bf16[128,32,128]{2,1,0:T(8,128)(2,1)S(1)} %bitcast.20), channel_id=1, replica_groups=mesh['y_hi'=2,'y_lo'=2,'z_lo'=2,'x_hi'=2,'x_lo'=2,'z_hi'=2,'core'=2] {'y..., dimensions={0} | all-to-all | bytes 2097152 | tf_op jit(solution)/shard_map/all_to_all | solution.py:277
  32.7 0.0 copy-done.1
  32.7 1.1 %shard_map.74 = bf16[2048,128]{1,0:T(8,128)(2,1)S(1)} custom-call(bf16[4096,128]{1,0:T(8,128)(2,1)S(1)} %bitcast.12, bf16[512,512]{1,0:T(8,128)(2,1)S(1)} %copy-done.1), custom_call_target="tpu_custom_call" | custom-call | tf_op jit(solution)/shard_map/pallas_call | solution.py:257
  33.8 0.0 copy-start
  33.8 0.0 copy-start.2
  33.8 0.0 copy-start.3
  33.8 0.0 copy-start.4
  33.8 17.8 %all_to_all.21 = bf16[128,16,128]{2,1,0:T(8,128)(2,1)S(1)} all-to-all(bf16[128,16,128]{2,1,0:T(8,128)(2,1)S(1)} %bitcast.16), channel_id=1, replica_groups=mesh['y_hi'=2,'y_lo'=2,'z_lo'=2,'x_hi'=2,'x_lo'=2,'z_hi'=2,'core'=2] {'y..., dimensions={0} | all-to-all | bytes 1048576 | tf_op jit(solution)/shard_map/all_to_all | solution.py:277
  51.6 0.0 copy-done
  51.6 0.0 copy-done.2
  51.6 0.0 copy-done.3
  51.6 0.0 copy-done.4
  51.6 1.8 %shard_map.75 = (bf16[2048,128]{1,0:T(8,128)(2,1)S(1)}, bf16[128,2,16,128]{3,2,1,0:T(8,128)(2,1)S(1)}, f32[2048,128]{1,0:T(8,128)S(1)}) custom-call(bf16[2048,128]{1,0:T(8,128)(2,1)S(1)} %bitcast.13, bf16[2048,128]{1,0:T(8,128)(2,1)S(1)} %bitcast.18, f32[2048,128]{1,0:T(8,128)S(1)} %get-tuple-element.12.gate_ref, bf16[2,128,128]{2,1,0:T(8,128)(2,1)S(1)} %copy-done.3, ...), custom_call_target="tpu_custom_call" | custom-call | tf_op jit(solution)/shard_map/pallas_call | solution.py:257
  53.4 23.0 %all_to_all.22 = bf16[128,32,128]{2,1,0:T(8,128)(2,1)S(1)} all-to-all(bf16[128,32,128]{2,1,0:T(8,128)(2,1)S(1)} %bitcast.19), channel_id=1, replica_groups=mesh['y_hi'=2,'y_lo'=2,'z_lo'=2,'x_hi'=2,'x_lo'=2,'z_hi'=2,'core'=2] {'y..., dimensions={0} | all-to-all | bytes 2097152 | tf_op jit(solution)/shard_map/all_to_all | solution.py:277
  76.4 1.0 %shard_map.76 = bf16[2048,128]{1,0:T(8,128)(2,1)S(1)} custom-call(bf16[4096,128]{1,0:T(8,128)(2,1)S(1)} %bitcast.11, bf16[512,512]{1,0:T(8,128)(2,1)S(1)} %copy-done.1), custom_call_target="tpu_custom_call" | custom-call | tf_op jit(solution)/shard_map/pallas_call | solution.py:257
  77.5 17.6 %all_to_all.23 = bf16[128,16,128]{2,1,0:T(8,128)(2,1)S(1)} all-to-all(bf16[128,16,128]{2,1,0:T(8,128)(2,1)S(1)} %bitcast.15), channel_id=1, replica_groups=mesh['y_hi'=2,'y_lo'=2,'z_lo'=2,'x_hi'=2,'x_lo'=2,'z_hi'=2,'core'=2] {'y..., dimensions={0} | all-to-all | bytes 1048576 | tf_op jit(solution)/shard_map/all_to_all | solution.py:277
  95.1 1.4 %shard_map.77 = bf16[4,16,32,128]{3,2,1,0:T(8,128)(2,1)} custom-call(bf16[2048,128]{1,0:T(8,128)(2,1)S(1)} %bitcast.14, bf16[2048,128]{1,0:T(8,128)(2,1)S(1)} %get-tuple-element.15.pair_ref, f32[2048,128]{1,0:T(8,128)S(1)} %get-tuple-element.16.gate_ref, bf16[2,128,128]{2,1,0:T(8,128)(2,1)S(1)} %copy-done.3, f32[2,2,128]{2,1,0:T(2,128)S(1)} %get-tuple-element.13.gain_ref), custom_call_target="tpu_custom_call" | custom-call | tf_op jit(solution)/shard_map/pallas_call | solution.py:257
Async XLA Ops:
  2.4 30.3 %copy-start.1 = (bf16[512,512]{1,0:T(8,128)(2,1)S(1)}, bf16[512,512]{1,0:T(8,128)(2,1)}, u32[]{:S(2)}) copy-start(bf16[512,512]{1,0:T(8,128)(2,1)} %constant.2.clone.regroup_ref) | copy-start | bytes 1572868
  33.8 17.8 %copy-start = (bf16[64,32,128]{2,1,0:T(8,128)(2,1)S(1)}, bf16[64,32,128]{2,1,0:T(8,128)(2,1)}, u32[]{:S(2)}) copy-start(bf16[64,32,128]{2,1,0:T(8,128)(2,1)} %param.7) | copy-start | bytes 1572868
  33.8 17.8 %copy-start.2 = (bf16[2,2,2,128,128]{4,3,2,1,0:T(8,128)(2,1)S(1)}, bf16[2,2,2,128,128]{4,3,2,1,0:T(8,128)(2,1)}, u32[]{:S(2)}) copy-start(bf16[2,2,2,128,128]{4,3,2,1,0:T(8,128)(2,1)} %param.8) | copy-start | bytes 786436
  33.8 17.8 %copy-start.3 = (bf16[2,128,128]{2,1,0:T(8,128)(2,1)S(1)}, bf16[2,128,128]{2,1,0:T(8,128)(2,1)}, u32[]{:S(2)}) copy-start(bf16[2,128,128]{2,1,0:T(8,128)(2,1)} %out_weight_ref.3) | copy-start | bytes 196612
  33.8 17.8 %copy-start.4 = (bf16[2,128,128]{2,1,0:T(8,128)(2,1)S(1)}, bf16[2,128,128]{2,1,0:T(8,128)(2,1)}, u32[]{:S(2)}) copy-start(bf16[2,128,128]{2,1,0:T(8,128)(2,1)} %rest_1_.1) | copy-start | bytes 196612

commit v7 on v4

--- a/solution.py
+++ b/solution.py
@@ -94,7 +94,7 @@
         return dot(side_by_side(normed_ref, n), weight, ((1,), (0,)))
 
     def gate(n, values):
-        values = jnp.tanh(values)
+        values = jnp.tanh(values).astype(BF16)
         gate_ref[n : n + 512, :] = values[:, :128]
         gate_ref[n + 512 : n + 1024, :] = values[:, 128:]
 
@@ -122,17 +122,17 @@
     wt_ref, centred_ref, normed_ref, half_ref, sems,
 ):
     copies = [
+        pltpu.make_async_copy(pair_hbm, pair_ref, sems.at[1]),
         pltpu.make_async_copy(side_hbm.at[pl.ds(0, 4)], side_ref, sems.at[0]),
-        pltpu.make_async_copy(pair_hbm, pair_ref, sems.at[1]),
         pltpu.make_async_copy(gate_weight_hbm.at[0], gate_weight_ref, sems.at[2]),
         pltpu.make_async_copy(gain_hbm, gain_ref.at[0], sems.at[3]),
         pltpu.make_async_copy(out_gain_hbm, gain_ref.at[1], sems.at[4]),
     ]
     for copy in copies:
         copy.start()
-    copies[0].wait()
+    copies[1].wait()
     fill_weights(side_ref, wt_ref, 0)
-    for copy in copies[1:]:
+    for copy in copies[:1] + copies[2:]:
         copy.wait()
     project(
         pair_ref, gain_ref[0, 0:1, :], wt_ref, gate_weight_ref[...],
@@ -242,7 +242,7 @@
         changes = dot(out_normed[s - 2].reshape(256, 128), weight, ((0,), (0,)))
         for n in range(2):
             change = changes[:, 128 * n : 128 * n + 128].reshape(4, 32, 128)
-            before, gate = slabs[0][:, s - 2 + n].astype(F32), slabs[1][:, s - 2 + n]
+            before, gate = slabs[0][:, s - 2 + n].astype(F32), slabs[1][:, s - 2 + n].astype(F32)
             slabs[2][:, s - 2 + n] = (before + (change + change * gate)).astype(BF16)
         if update == 1 and s % 4 == 0:
             part = pl.ds(s - 4, 4)
@@ -273,7 +273,7 @@
 SIDES = ((128, 2, 16, 128), BF16)
 MIXED = ((2048, 128), BF16)
 PAIR = ((2048, 128), BF16)
-GATE = ((2048, 128), F32)
+GATE = ((2048, 128), BF16)
 GAIN = ((2, 2, 128), F32)
 PROJECT_SCRATCH = [((512, 128), BF16), ((1024, 256), F32), ((2048, 128), BF16), ((5120, 128), F32)]
 

time: 96.7 us -> 96.7 us (level)
  no operation moved by 1% of the time
where the time goes in v7:
time: 96.7 us; the launch traced here: 96.5 us
  blocking collectives  88.6 us (92%)
  Pallas kernels  7.77 us (8%)
    all_to_all x4, blocking collectives, exchange(): lax.all_to_all(pieces, ORDER, split_axis=0, concat_axis=0, tiled=True)  88.6 us
    pallas_call x5, Pallas kernels, call(): pl.pallas_call(kernel, out_shape=[jax.ShapeDtypeStruct(*one) for one in o...  7.77 us

profile of v7, /device:TPU:1, one launch (start us, length us, event | category | flops | bytes accessed | tf_op | source)
XLA Modules:
  0.0 96.5 jit_solution(12573577967190580198)
XLA Ops:
  0.0 2.5 %shard_map.73 = (bf16[128,2,16,128]{3,2,1,0:T(8,128)(2,1)S(1)}, bf16[2048,128]{1,0:T(8,128)(2,1)S(1)}, f32[2,2,128]{2,1,0:T(2,128)S(1)}) custom-call(bf16[2048,128]{1,0:T(8,128)(2,1)} %bitcast.15, bf16[8,128,128]{2,1,0:T(8,128)(2,1)} %bitcast.19, bf16[2,128,128]{2,1,0:T(8,128)(2,1)} %rest_1_.1, f32[2,128]{1,0:T(2,128)} %gain_hbm.1, f32[2,128]{1,0:T(2,128)} %out_gain_hbm.1), custom_call_target="tpu_custom_call" | custom-call | tf_op jit(solution)/shard_map/pallas_call | solution.py:263
  2.5 0.0 copy-start.1
  2.5 30.2 %all_to_all.20 = bf16[128,32,128]{2,1,0:T(8,128)(2,1)S(1)} all-to-all(bf16[128,32,128]{2,1,0:T(8,128)(2,1)S(1)} %bitcast.22), channel_id=1, replica_groups=mesh['y_hi'=2,'y_lo'=2,'z_lo'=2,'x_hi'=2,'x_lo'=2,'z_hi'=2,'core'=2] {'y..., dimensions={0} | all-to-all | bytes 2097152 | tf_op jit(solution)/shard_map/all_to_all | solution.py:283
  32.7 0.0 copy-done.1
  32.7 1.1 %shard_map.74 = bf16[2048,128]{1,0:T(8,128)(2,1)S(1)} custom-call(bf16[4096,128]{1,0:T(8,128)(2,1)S(1)} %bitcast.12, bf16[512,512]{1,0:T(8,128)(2,1)S(1)} %copy-done.1), custom_call_target="tpu_custom_call" | custom-call | tf_op jit(solution)/shard_map/pallas_call | solution.py:263
  33.8 0.0 copy-start
  33.8 0.0 copy-start.2
  33.8 0.0 copy-start.3
  33.8 0.0 copy-start.4
  33.9 17.8 %all_to_all.21 = bf16[128,16,128]{2,1,0:T(8,128)(2,1)S(1)} all-to-all(bf16[128,16,128]{2,1,0:T(8,128)(2,1)S(1)} %bitcast.18), channel_id=1, replica_groups=mesh['y_hi'=2,'y_lo'=2,'z_lo'=2,'x_hi'=2,'x_lo'=2,'z_hi'=2,'core'=2] {'y..., dimensions={0} | all-to-all | bytes 1048576 | tf_op jit(solution)/shard_map/all_to_all | solution.py:283
  51.6 0.0 copy-done
  51.6 0.0 copy-done.2
  51.6 0.0 copy-done.3
  51.6 0.0 copy-done.4
  51.6 1.8 %shard_map.75 = (bf16[2048,128]{1,0:T(8,128)(2,1)S(1)}, bf16[128,2,16,128]{3,2,1,0:T(8,128)(2,1)S(1)}, bf16[2048,128]{1,0:T(8,128)(2,1)S(1)}) custom-call(bf16[2048,128]{1,0:T(8,128)(2,1)S(1)} %bitcast.13, bf16[2048,128]{1,0:T(8,128)(2,1)S(1)} %bitcast.16, bf16[2048,128]{1,0:T(8,128)(2,1)S(1)} %get-tuple-element.12.gate_ref, ...), custom_call_target="tpu_custom_call" | custom-call | tf_op jit(solution)/shard_map/pallas_call | solution.py:263
  53.5 23.0 %all_to_all.22 = bf16[128,32,128]{2,1,0:T(8,128)(2,1)S(1)} all-to-all(bf16[128,32,128]{2,1,0:T(8,128)(2,1)S(1)} %bitcast.21), channel_id=1, replica_groups=mesh['y_hi'=2,'y_lo'=2,'z_lo'=2,'x_hi'=2,'x_lo'=2,'z_hi'=2,'core'=2] {'y..., dimensions={0} | all-to-all | bytes 2097152 | tf_op jit(solution)/shard_map/all_to_all | solution.py:283
  76.5 1.0 %shard_map.76 = bf16[2048,128]{1,0:T(8,128)(2,1)S(1)} custom-call(bf16[4096,128]{1,0:T(8,128)(2,1)S(1)} %bitcast.11, bf16[512,512]{1,0:T(8,128)(2,1)S(1)} %copy-done.1), custom_call_target="tpu_custom_call" | custom-call | tf_op jit(solution)/shard_map/pallas_call | solution.py:263
  77.5 17.6 %all_to_all.23 = bf16[128,16,128]{2,1,0:T(8,128)(2,1)S(1)} all-to-all(bf16[128,16,128]{2,1,0:T(8,128)(2,1)S(1)} %bitcast.17), channel_id=1, replica_groups=mesh['y_hi'=2,'y_lo'=2,'z_lo'=2,'x_hi'=2,'x_lo'=2,'z_hi'=2,'core'=2] {'y..., dimensions={0} | all-to-all | bytes 1048576 | tf_op jit(solution)/shard_map/all_to_all | solution.py:283
  95.1 1.4 %shard_map.77 = bf16[4,16,32,128]{3,2,1,0:T(8,128)(2,1)} custom-call(bf16[2048,128]{1,0:T(8,128)(2,1)S(1)} %bitcast.14, bf16[2048,128]{1,0:T(8,128)(2,1)S(1)} %get-tuple-element.15.pair_ref, bf16[2048,128]{1,0:T(8,128)(2,1)S(1)} %get-tuple-element.16.gate_ref, bf16[2,128,128]{2,1,0:T(8,128)(2,1)S(1)} %copy-done.3, f32[2,2,128]{2,1,0:T(2,128)S(1)} %get-tuple-element.13.gain_ref), custom_call_target="tpu_custom_call" | custom-call | tf_op jit(solution)/shard_map/pallas_call | solution.py:263
Async XLA Ops:
  2.5 30.2 %copy-start.1 = (bf16[512,512]{1,0:T(8,128)(2,1)S(1)}, bf16[512,512]{1,0:T(8,128)(2,1)}, u32[]{:S(2)}) copy-start(bf16[512,512]{1,0:T(8,128)(2,1)} %constant.2.clone.regroup_ref) | copy-start | bytes 1572868
  33.8 17.8 %copy-start = (bf16[64,32,128]{2,1,0:T(8,128)(2,1)S(1)}, bf16[64,32,128]{2,1,0:T(8,128)(2,1)}, u32[]{:S(2)}) copy-start(bf16[64,32,128]{2,1,0:T(8,128)(2,1)} %param.7) | copy-start | bytes 1572868
  33.8 17.8 %copy-start.2 = (bf16[2,2,2,128,128]{4,3,2,1,0:T(8,128)(2,1)S(1)}, bf16[2,2,2,128,128]{4,3,2,1,0:T(8,128)(2,1)}, u32[]{:S(2)}) copy-start(bf16[2,2,2,128,128]{4,3,2,1,0:T(8,128)(2,1)} %param.8) | copy-start | bytes 786436
  33.8 17.8 %copy-start.3 = (bf16[2,128,128]{2,1,0:T(8,128)(2,1)S(1)}, bf16[2,128,128]{2,1,0:T(8,128)(2,1)}, u32[]{:S(2)}) copy-start(bf16[2,128,128]{2,1,0:T(8,128)(2,1)} %out_weight_ref.3) | copy-start | bytes 196612
  33.8 17.8 %copy-start.4 = (bf16[2,128,128]{2,1,0:T(8,128)(2,1)S(1)}, bf16[2,128,128]{2,1,0:T(8,128)(2,1)}, u32[]{:S(2)}) copy-start(bf16[2,128,128]{2,1,0:T(8,128)(2,1)} %rest_1_.1) | copy-start | bytes 196612

commit v8 on v4

--- a/solution.py
+++ b/solution.py
@@ -168,6 +168,7 @@
             tiles.append(jnp.concatenate([in_ref[32 * m + 16 * side : 32 * m + 16 * side + 16, :] for m in numbers], axis=0))
         return jnp.concatenate(tiles, axis=1)
 
+    side, full_ref = ((0, left_ref), (1, right_ref))[update]
     for half in range(2):
         if update == 0:
             places = [(4 * half + r, block) for r in range(4) for block in range(4)]
@@ -185,16 +186,15 @@
                     row = 128 * (2 * half + block)
                     tile = regrouped[128 * g : 128 * g + 128, 128 * block : 128 * block + 128]
                     left_ref[row : row + 128, 128 * g : 128 * g + 128] = tile
-    side, full_ref = ((0, left_ref), (1, right_ref))[update]
-    places = [(r, block) for r in range(8) for block in range(4)]
-    groups = []
-    for r, block in places:
-        numbers = [device_number(r, 4 * block + n) for n in range(4)]
-        groups.append([in_ref[32 * m + 16 * side : 32 * m + 16 * side + 16, :] for m in numbers])
-    for (r, block), tiles in zip(places, swap_groups(groups, low, even)):
-        for g, tile in enumerate(tiles):
-            row = r * 64 + g * 16 if update == 0 else g * 128 + r * 16
-            full_ref[row : row + 16, 128 * block : 128 * block + 128] = tile
+        places = [(r, block) for r in range(4 * half, 4 * half + 4) for block in range(4)]
+        groups = []
+        for r, block in places:
+            numbers = [device_number(r, 4 * block + n) for n in range(4)]
+            groups.append([in_ref[32 * m + 16 * side : 32 * m + 16 * side + 16, :] for m in numbers])
+        for (r, block), tiles in zip(places, swap_groups(groups, low, even)):
+            for g, tile in enumerate(tiles):
+                row = r * 64 + g * 16 if update == 0 else g * 128 + r * 16
+                full_ref[row : row + 16, 128 * block : 128 * block + 128] = tile
     products = []
     for half in range(2):
         part = slice(256 * half, 256 * half + 256)

time: 96.7 us -> 96.6 us (level)
  no operation moved by 1% of the time
where the time goes in v8:
time: 96.6 us; the launch traced here: 96.4 us
  blocking collectives  88.6 us (92%)
  Pallas kernels  7.7 us (8%)
    all_to_all x4, blocking collectives, exchange(): lax.all_to_all(pieces, ORDER, split_axis=0, concat_axis=0, tiled=True)  88.6 us
    pallas_call x5, Pallas kernels, call(): pl.pallas_call(kernel, out_shape=[jax.ShapeDtypeStruct(*one) for one in o...  7.7 us

profile of v8, /device:TPU:1, one launch (start us, length us, event | category | flops | bytes accessed | tf_op | source)
XLA Modules:
  0.0 96.4 jit_solution(3780494445040177566)
XLA Ops:
  0.0 2.4 %shard_map.73 = (bf16[128,2,16,128]{3,2,1,0:T(8,128)(2,1)S(1)}, f32[2048,128]{1,0:T(8,128)S(1)}, f32[2,2,128]{2,1,0:T(2,128)S(1)}) custom-call(bf16[2048,128]{1,0:T(8,128)(2,1)} %bitcast.17, bf16[8,128,128]{2,1,0:T(8,128)(2,1)} %bitcast.21, bf16[2,128,128]{2,1,0:T(8,128)(2,1)} %rest_1_.1, f32[2,128]{1,0:T(2,128)} %gain_hbm.1, f32[2,128]{1,0:T(2,128)} %out_gain_hbm.1), custom_call_target="tpu_custom_call" | custom-call | tf_op jit(solution)/shard_map/pallas_call | solution.py:263
  2.4 0.0 copy-start.1
  2.4 30.2 %all_to_all.20 = bf16[128,32,128]{2,1,0:T(8,128)(2,1)S(1)} all-to-all(bf16[128,32,128]{2,1,0:T(8,128)(2,1)S(1)} %bitcast.20), channel_id=1, replica_groups=mesh['y_hi'=2,'y_lo'=2,'z_lo'=2,'x_hi'=2,'x_lo'=2,'z_hi'=2,'core'=2] {'y..., dimensions={0} | all-to-all | bytes 2097152 | tf_op jit(solution)/shard_map/all_to_all | solution.py:283
  32.7 0.0 copy-done.1
  32.7 1.1 %shard_map.74 = bf16[2048,128]{1,0:T(8,128)(2,1)S(1)} custom-call(bf16[4096,128]{1,0:T(8,128)(2,1)S(1)} %bitcast.12, bf16[512,512]{1,0:T(8,128)(2,1)S(1)} %copy-done.1), custom_call_target="tpu_custom_call" | custom-call | tf_op jit(solution)/shard_map/pallas_call | solution.py:263
  33.7 0.0 copy-start
  33.8 0.0 copy-start.2
  33.8 0.0 copy-start.3
  33.8 0.0 copy-start.4
  33.8 17.8 %all_to_all.21 = bf16[128,16,128]{2,1,0:T(8,128)(2,1)S(1)} all-to-all(bf16[128,16,128]{2,1,0:T(8,128)(2,1)S(1)} %bitcast.16), channel_id=1, replica_groups=mesh['y_hi'=2,'y_lo'=2,'z_lo'=2,'x_hi'=2,'x_lo'=2,'z_hi'=2,'core'=2] {'y..., dimensions={0} | all-to-all | bytes 1048576 | tf_op jit(solution)/shard_map/all_to_all | solution.py:283
  51.6 0.0 copy-done
  51.6 0.0 copy-done.2
  51.6 0.0 copy-done.3
  51.6 0.0 copy-done.4
  51.6 1.8 %shard_map.75 = (bf16[2048,128]{1,0:T(8,128)(2,1)S(1)}, bf16[128,2,16,128]{3,2,1,0:T(8,128)(2,1)S(1)}, f32[2048,128]{1,0:T(8,128)S(1)}) custom-call(bf16[2048,128]{1,0:T(8,128)(2,1)S(1)} %bitcast.13, bf16[2048,128]{1,0:T(8,128)(2,1)S(1)} %bitcast.18, f32[2048,128]{1,0:T(8,128)S(1)} %get-tuple-element.12.gate_ref, bf16[2,128,128]{2,1,0:T(8,128)(2,1)S(1)} %copy-done.3, ...), custom_call_target="tpu_custom_call" | custom-call | tf_op jit(solution)/shard_map/pallas_call | solution.py:263
  53.4 23.0 %all_to_all.22 = bf16[128,32,128]{2,1,0:T(8,128)(2,1)S(1)} all-to-all(bf16[128,32,128]{2,1,0:T(8,128)(2,1)S(1)} %bitcast.19), channel_id=1, replica_groups=mesh['y_hi'=2,'y_lo'=2,'z_lo'=2,'x_hi'=2,'x_lo'=2,'z_hi'=2,'core'=2] {'y..., dimensions={0} | all-to-all | bytes 2097152 | tf_op jit(solution)/shard_map/all_to_all | solution.py:283
  76.4 1.0 %shard_map.76 = bf16[2048,128]{1,0:T(8,128)(2,1)S(1)} custom-call(bf16[4096,128]{1,0:T(8,128)(2,1)S(1)} %bitcast.11, bf16[512,512]{1,0:T(8,128)(2,1)S(1)} %copy-done.1), custom_call_target="tpu_custom_call" | custom-call | tf_op jit(solution)/shard_map/pallas_call | solution.py:263
  77.4 17.6 %all_to_all.23 = bf16[128,16,128]{2,1,0:T(8,128)(2,1)S(1)} all-to-all(bf16[128,16,128]{2,1,0:T(8,128)(2,1)S(1)} %bitcast.15), channel_id=1, replica_groups=mesh['y_hi'=2,'y_lo'=2,'z_lo'=2,'x_hi'=2,'x_lo'=2,'z_hi'=2,'core'=2] {'y..., dimensions={0} | all-to-all | bytes 1048576 | tf_op jit(solution)/shard_map/all_to_all | solution.py:283
  95.1 1.4 %shard_map.77 = bf16[4,16,32,128]{3,2,1,0:T(8,128)(2,1)} custom-call(bf16[2048,128]{1,0:T(8,128)(2,1)S(1)} %bitcast.14, bf16[2048,128]{1,0:T(8,128)(2,1)S(1)} %get-tuple-element.15.pair_ref, f32[2048,128]{1,0:T(8,128)S(1)} %get-tuple-element.16.gate_ref, bf16[2,128,128]{2,1,0:T(8,128)(2,1)S(1)} %copy-done.3, f32[2,2,128]{2,1,0:T(2,128)S(1)} %get-tuple-element.13.gain_ref), custom_call_target="tpu_custom_call" | custom-call | tf_op jit(solution)/shard_map/pallas_call | solution.py:263
Async XLA Ops:
  2.4 30.2 %copy-start.1 = (bf16[512,512]{1,0:T(8,128)(2,1)S(1)}, bf16[512,512]{1,0:T(8,128)(2,1)}, u32[]{:S(2)}) copy-start(bf16[512,512]{1,0:T(8,128)(2,1)} %constant.2.clone.regroup_ref) | copy-start | bytes 1572868
  33.7 17.8 %copy-start = (bf16[64,32,128]{2,1,0:T(8,128)(2,1)S(1)}, bf16[64,32,128]{2,1,0:T(8,128)(2,1)}, u32[]{:S(2)}) copy-start(bf16[64,32,128]{2,1,0:T(8,128)(2,1)} %param.7) | copy-start | bytes 1572868
  33.8 17.8 %copy-start.2 = (bf16[2,2,2,128,128]{4,3,2,1,0:T(8,128)(2,1)S(1)}, bf16[2,2,2,128,128]{4,3,2,1,0:T(8,128)(2,1)}, u32[]{:S(2)}) copy-start(bf16[2,2,2,128,128]{4,3,2,1,0:T(8,128)(2,1)} %param.8) | copy-start | bytes 786436
  33.8 17.8 %copy-start.3 = (bf16[2,128,128]{2,1,0:T(8,128)(2,1)S(1)}, bf16[2,128,128]{2,1,0:T(8,128)(2,1)}, u32[]{:S(2)}) copy-start(bf16[2,128,128]{2,1,0:T(8,128)(2,1)} %out_weight_ref.3) | copy-start | bytes 196612
  33.8 17.8 %copy-start.4 = (bf16[2,128,128]{2,1,0:T(8,128)(2,1)S(1)}, bf16[2,128,128]{2,1,0:T(8,128)(2,1)}, u32[]{:S(2)}) copy-start(bf16[2,128,128]{2,1,0:T(8,128)(2,1)} %rest_1_.1) | copy-start | bytes 196612
